TPU v7x, 256 devices: a whole 4x4x8 slice. The times are simulated.
256 devices in a mesh: row: 16 (over y, z_hi), col: 16 (over x, z_lo, core).
Axes of the slice: x: 4, y: 4, z: 8 (z_hi: 4, z_lo: 2; z = z_hi * 2 + z_lo), core: 2. Of those that a mesh axis runs over, the one named last changes fastest.
Arguments:
- features: bfloat16 [65536, 512], P(('row', 'col')), may hold values from -8 to 8
- w_self: bfloat16 [512, 512], replicated, may hold values from -0.25 to 0.25
- w_neigh: bfloat16 [512, 512], replicated, may hold values from -0.25 to 0.25
- cotangent: bfloat16 [65536, 512], P(('row', 'col')), may hold values from -8 to 8
- tile_values: bfloat16 [12288, 256, 256], P(('row', 'col')), as said below
- tile_dst: int32 [12288], P(('row', 'col')), may hold values from 0 to 15
- tile_src: int32 [12288], P(('row', 'col')), may hold values from 0 to 15
- tile_count: int32 [256], P(('row', 'col')), may hold values from 1 to 47, as said below
Outputs:
- output: bfloat16 [65536, 512], P(('row', 'col'))
- grad_features: bfloat16 [65536, 512], P(('row', 'col'))
- grad_self: float32 [512, 512], replicated
- grad_neigh: float32 [512, 512], replicated
Inputs may be any that keep to these rules, and one draw needn't show every extreme that they name: `tile_count`: A is symmetric: a live slot at tiles (I, J) has a live slot at (J, I) with the transposed values, and each device's diagonal tile of its own node block (I = J = d) is live. Live slots come first, each (a, b) once; the busiest device has exactly 47 live slots. `tile_values`: entries are nonnegative; the diagonal of every node's own diagonal tile is 1 or more.
All inputs are finite; a program needn't handle non-finite values.
Results may differ from a plain program's by a relative error of at most 0.0085.
Values may be sent and summed in bfloat16 or wider, within the bound.
No kernel may reach another device: no remote copies, remote signals or barrier semaphores. Data moves between devices by JAX's collectives and lax.ppermute only.
A program may use at most 128 MiB of HBM per device.

v0:
```python
import jax
import jax.numpy as jnp
from jax import lax
from jax.sharding import PartitionSpec as P


def spread_tiles(tile_values, targets_all, anchors_all, number, sources, out_tiles, pattern):
    tile_edge = tile_values.shape[1]
    feature_width = sources.shape[1]
    source_tiles = sources.reshape(-1, tile_edge, feature_width)
    totals = jnp.zeros((out_tiles, tile_edge, feature_width), jnp.float32)
    rounds = (number + 3) // 4

    def visit(position, totals):
        offset = position * 4
        blocks = lax.dynamic_slice_in_dim(tile_values, offset, 4, 0)
        targets = lax.dynamic_slice_in_dim(targets_all, offset, 4, 0)
        anchors = lax.dynamic_slice_in_dim(anchors_all, offset, 4, 0)
        active = (offset + jnp.arange(4, dtype=jnp.int32) < number).astype(jnp.float32)
        product = jnp.einsum(
            pattern, blocks, source_tiles[anchors], preferred_element_type=jnp.float32
        )
        return totals.at[targets].add(product * active[:, None, None])

    totals = lax.fori_loop(0, rounds, visit, totals)
    return totals.reshape(out_tiles * tile_edge, feature_width)


def shards(features, w_self, w_neigh, cotangent, tile_values, tile_dst, tile_src, tile_count):
    number = tile_count[0]
    tile_edge = tile_values.shape[1]
    row_count = lax.axis_size("row")
    col_count = lax.axis_size("col")
    gathered = lax.all_gather(features, "row", axis=0, tiled=True)
    partial_value = spread_tiles(
        tile_values, tile_dst, tile_src, number, gathered, col_count, "tij,tjf->tif"
    )
    active = (jnp.arange(tile_values.shape[0], dtype=jnp.int32) < number).astype(jnp.float32)
    tile_sums = jnp.sum(tile_values, axis=2, dtype=jnp.float32) * active[:, None]
    row_weight = (
        jnp.zeros((col_count, tile_edge), jnp.float32).at[tile_dst].add(tile_sums).reshape(-1)
    )
    summed, degree = (
        lax.psum_scatter(partial_value, "col", scatter_dimension=0, tiled=True),
        lax.psum_scatter(row_weight, "col", scatter_dimension=0, tiled=True),
    )
    neighbor_mean = (summed / degree[:, None]).astype(jnp.bfloat16)
    preact = jnp.dot(features, w_self, preferred_element_type=jnp.float32) + jnp.dot(
        neighbor_mean, w_neigh, preferred_element_type=jnp.float32
    )
    sigmoid_part = jax.nn.sigmoid(preact)
    output = (preact * sigmoid_part).astype(jnp.bfloat16)
    grad_pre = (
        cotangent.astype(jnp.float32) * sigmoid_part * (1.0 + preact * (1.0 - sigmoid_part))
    ).astype(jnp.bfloat16)
    contract_rows = (((0,), (0,)), ((), ()))
    contract_cols = (((1,), (1,)), ((), ()))
    local_self = lax.dot_general(
        features, grad_pre, contract_rows, preferred_element_type=jnp.float32
    )
    local_neigh = lax.dot_general(
        neighbor_mean, grad_pre, contract_rows, preferred_element_type=jnp.float32
    )
    grad_self, grad_neigh = lax.psum((local_self, local_neigh), ("row", "col"))
    scaled_back = (
        lax.dot_general(grad_pre, w_neigh, contract_cols, preferred_element_type=jnp.float32)
        / degree[:, None]
    ).astype(jnp.bfloat16)
    own_term = lax.dot_general(grad_pre, w_self, contract_cols, preferred_element_type=jnp.float32)
    row_values = lax.all_gather(scaled_back, "col", axis=0, tiled=True)
    partial_back = spread_tiles(
        tile_values, tile_src, tile_dst, number, row_values, row_count, "tji,tjf->tif"
    )
    returned = lax.psum_scatter(
        partial_back.astype(jnp.bfloat16), "row", scatter_dimension=0, tiled=True
    ).astype(jnp.float32)
    grad_features = (own_term + returned).astype(jnp.bfloat16)
    return (output, grad_features, grad_self, grad_neigh)


def solution(mesh):
    return jax.shard_map(
        shards,
        mesh=mesh,
        in_specs=(
            P(("row", "col"), None),
            P(),
            P(),
            P(("row", "col"), None),
            P(("row", "col"), None, None),
            P(("row", "col")),
            P(("row", "col")),
            P(("row", "col")),
        ),
        out_specs=(P(("row", "col"), None), P(("row", "col"), None), P(), P()),
        check_vma=False,
    )
```

profile of v0, /device:TPU:1, one launch (start us, length us, event | category | flops | bytes accessed | tf_op | source)
XLA Modules:
  0.0 736.4 jit_solution(16935088260497957290)
XLA Ops:
  8.7 80.4 %all-gather.3.cloned.1.call-done = bf16[4096,512]{1,0:T(8,128)(2,1)} async-done(((bf16[256,512]{1,0:T(8,128)(2,1)}), bf16[4096,512]{1,0:T(8,128)(2,1)}) %all-gather.3.cloned.1.call-update) | async-done | bytes 4194320 | tf_op jit(solution)/shard_map/all_gather | solution.py:34
  89.0 4.3 broadcast.40.clone
  93.3 42.2 %while.20 = (s32[]{:T(128)}, f32[16,256,512]{2,1,0:T(8,128)}, s32[]{:T(128)}, s32[48]{0:T(128)S(1)}, bf16[48,256,256]{2,1,0:T(8,128)(2,1)}, /*index=5*/s32[48]{0...) while((s32[]{:T(128)}, f32[16,256,512]{2,1,0:T(8,128)}, ...), condition=%wide.region_2.3_spmd, body=%wide.region_0.2_spmd.sunk | while | flops 269485088 | bytes 12063051 | solution.py:25
  93.4 3.8 gather_fusion
  99.7 4.1 scatter_fusion
  103.8 3.8 gather_fusion
  110.1 4.2 scatter_fusion
  114.4 3.8 gather_fusion
  120.7 4.3 scatter_fusion
  125.1 3.8 gather_fusion
  131.3 4.1 scatter_fusion
  135.6 4.6 convert_reduce_fusion
  142.4 80.9 %all-reduce = f32[4096]{0:T(1024)S(1)} all-reduce(f32[4096]{0:T(1024)S(1)} %bitcast.32), channel_id=3, replica_groups=mesh['row'=16,'col'=16] {'col'}, use_global_device_ids=true, to_apply=%region_6.7.clone | all-reduce | flops 4096 | bytes 32768
  223.7 93.3 %reduce-scatter.3.cloned.1.call-done = f32[256,512]{1,0:T(8,128)} async-done(((f32[4096,512]{1,0:T(8,128)}), f32[256,512]{1,0:T(8,128)}) %reduce-scatter.3.cloned.1.call-update) | async-done | bytes 524304 | tf_op jit(solution)/shard_map/reduce_scatter | solution.py:44
  316.9 2.4 multiply_convert_fusion
  323.2 37.9 %all-gather.5.cloned.1.call-done = bf16[4096,512]{1,0:T(8,128)(2,1)} async-done(((bf16[256,512]{1,0:T(8,128)(2,1)}), bf16[4096,512]{1,0:T(8,128)(2,1)}) %all-gather.5.cloned.1.call-update) | async-done | bytes 4194320 | tf_op jit(solution)/shard_map/all_gather | solution.py:70
  361.1 4.3 broadcast.40
  365.3 43.0 %while.21 = (s32[]{:T(128)}, f32[16,256,512]{2,1,0:T(8,128)}, s32[]{:T(128)}, s32[48]{0:T(128)S(1)}, bf16[48,256,256]{2,1,0:T(8,128)(2,1)}, /*index=5*/s32[48]{0...) while((s32[]{:T(128)}, f32[16,256,512]{2,1,0:T(8,128)}, ...), condition=%wide.region_9.10_spmd, body=%wide.region_7.9_spmd.sunk | while | flops 269485088 | bytes 12063051 | solution.py:25
  365.4 3.8 gather_fusion.1
  371.8 4.4 scatter_fusion.1
  376.2 3.9 gather_fusion.1
  382.7 4.3 scatter_fusion.1
  387.1 3.8 gather_fusion.1
  393.5 4.3 scatter_fusion.1
  397.8 3.8 gather_fusion.1
  404.2 4.1 scatter_fusion.1
  408.3 6.0 convert_element_type.58
  414.3 212.5 %all-reduce.4.cloned.1.call-done = (f32[512,512]{0,1:T(8,128)}, f32[512,512]{1,0:T(8,128)}) async-done(((f32[512,512]{0,1:T(8,128)}, f32[512,512]{1,0:T(8,128)}), (f32[512,512]{0,1:T(8,128)}, f32[512,512]{1,0:T(8,128)})) %all-reduce.4.cloned.1.call-update) | async-done | bytes 2097168 | tf_op jit(solution)/shard_map/psum | solution.py:64
  626.8 2.5 copy.15
  629.3 96.3 %reduce-scatter.5.cloned.1.call-done = bf16[256,512]{1,0:T(8,128)(2,1)} async-done(((bf16[4096,512]{1,0:T(8,128)(2,1)}), bf16[256,512]{1,0:T(8,128)(2,1)}) %reduce-scatter.5.cloned.1.call-update) | async-done | bytes 262160 | tf_op jit(solution)/shard_map/reduce_scatter | solution.py:74
  725.6 2.0 fusion.4
  727.6 2.3 copy.36
  (68 shorter events, 27.3 us)
Async XLA Ops:
  7.2 309.8 %copy-start = (bf16[512,512]{1,0:T(8,128)(2,1)S(1)}, bf16[512,512]{1,0:T(8,128)(2,1)}, u32[]{:S(2)}) copy-start(bf16[512,512]{1,0:T(8,128)(2,1)} %param.14) | copy-start | bytes 1572868
  7.2 86.1 %copy-start.3 = (s32[48]{0:T(128)S(1)}, s32[48]{0:T(128)}, u32[]{:S(2)}) copy-start(s32[48]{0:T(128)} %param.17) | copy-start | bytes 580
  7.2 86.1 %copy-start.4 = (s32[48]{0:T(128)S(1)}, s32[48]{0:T(128)}, u32[]{:S(2)}) copy-start(s32[48]{0:T(128)} %param.18) | copy-start | bytes 580
  7.2 81.8 %all-gather.3.cloned.1.call-start = ((), (), s32[]{:S(2)}) async-start(), calls=%async_computation.2 | async-start | bytes 4456448 | tf_op jit(solution)/shard_map/all_gather | solution.py:34
  7.9 309.0 %reduce-scatter.3.cloned.1.call-start = ((), (), s32[]{:S(2)}) async-start(), calls=%async_computation.3 | async-start | bytes 8912896 | tf_op jit(solution)/shard_map/reduce_scatter | solution.py:44
  135.5 5.6 copy-start.7
  135.5 87.9 %copy-start.1 = (bf16[256,512]{1,0:T(8,128)(2,1)S(1)}, bf16[256,512]{1,0:T(8,128)(2,1)}, u32[]{:S(2)}) copy-start(bf16[256,512]{1,0:T(8,128)(2,1)} %param.12) | copy-start | bytes 786436
  135.5 87.9 %copy-start.2 = (bf16[512,512]{1,0:T(8,128)(2,1)S(1)}, bf16[512,512]{1,0:T(8,128)(2,1)}, u32[]{:S(2)}) copy-start(bf16[512,512]{1,0:T(8,128)(2,1)} %param.13) | copy-start | bytes 1572868
  135.5 181.5 %copy-start.6 = (bf16[256,512]{1,0:T(8,128)(2,1)S(1)}, bf16[256,512]{1,0:T(8,128)(2,1)}, u32[]{:S(2)}) copy-start(bf16[256,512]{1,0:T(8,128)(2,1)} %param.15) | copy-start | bytes 786436
  135.5 225.5 %all-gather.5.cloned.1.call-start = ((), (), s32[]{:S(2)}) async-start(), calls=%async_computation.4 | async-start | bytes 4456448 | tf_op jit(solution)/shard_map/all_gather | solution.py:70
  316.9 4.8 copy-start.5
  320.4 306.4 %all-reduce.4.cloned.1.call-start = ((), (), s32[]{:S(2)}) async-start(), calls=%async_computation.6 | async-start | bytes 4194304 | tf_op jit(solution)/shard_map/psum | solution.py:64
  323.1 402.5 %reduce-scatter.5.cloned.1.call-start = ((), (), s32[]{:S(2)}) async-start(), calls=%async_computation.5 | async-start | bytes 4456448 | tf_op jit(solution)/shard_map/reduce_scatter | solution.py:74
Sparse Core Ops, SparseCore 0:
  10.5 78.4 all-gather.2
  135.6 181.2 reduce-scatter.2
  320.5 40.5 all-gather.4
  367.0 259.7 all-reduce.3
  630.3 95.3 reduce-scatter.4
where the time goes:
time: 739 us; the launch traced here: 736 us
  waiting for transfers between devices  521 us (71%)
  blocking collectives  80.9 us (11%)
  other arithmetic  51.1 us (7%)
  local copies, waits for them, and re-layouts  44.6 us (6%)
  matrix products  23.2 us (3%)
  between operations  15.2 us (2%)
    psum x1, waiting for transfers between devices, shards(): grad_self, grad_neigh = lax.psum((local_self, local_neigh), ('row', 'col'))  212 us
    reduce_scatter x1, waiting for transfers between devices, shards(): lax.psum_scatter(partial_back.astype(jnp.bfloat16), 'row', scatter_dimens...  96.3 us
    reduce_scatter x1, waiting for transfers between devices, shards(): lax.psum_scatter(partial_value, 'col', scatter_dimension=0, tiled=True)  93.3 us
    unnamed x1, blocking collectives  80.9 us
    all_gather x1, waiting for transfers between devices, shards(): gathered = lax.all_gather(features, 'row', axis=0, tiled=True)  80.4 us
    all_gather x1, waiting for transfers between devices, shards(): row_values = lax.all_gather(scaled_back, 'col', axis=0, tiled=True)  37.9 us
    scatter-add x8, other arithmetic, visit(): return totals.at[targets].add(product * active[:, None, None])  33.8 us
    gather x8, local copies, waits for them, and re-layouts, visit(): source_tiles[anchors]  30.5 us
  transfers between devices with their start and end apart: 5, of which 5 were waited for; matrix products, arithmetic and copies ran while one was open for 9% of the time, Pallas kernels for 0%

commit v1 on v0

v1 whole, which is shorter than its diff:
```python
import functools

import jax
import jax.numpy as jnp
from jax import lax
from jax.experimental import pallas as pl
from jax.experimental.pallas import tpu as pltpu
from jax.sharding import PartitionSpec as P

MIB = 1 << 20
BOTH = ("row", "col")
CONTRACT_ROWS = (((0,), (0,)), ((), ()))
CONTRACT_COLS = (((1,), (1,)), ((), ()))

GATHER = (
    (("z", 1, 3), ("z", 3, 1), ("y", 1, 3), ("y", 3, 1)),
    (("y", 1, 3), ("y", 3, 1), ("z", 1, 3), ("z", 3, 1)),
)
ROWS = ((0, 176), (176, 80))
REDUCE = (
    (("x", 1, 3), ("x", 3, 1), ("l", 1, 1)),
    (("l", 1, 1), ("x", 1, 3), ("x", 3, 1)),
)
ROW_SUM = (("y", 1, 3), ("y", 3, 1), ("z", 1, 3), ("z", 3, 1))
AXES = ("y", "z", "x", "l", "c")
SIZES = (4, 4, 4, 2, 2)


def exchange(value, step):
    axis, *masks = step
    pairs = []
    for i in range(256):
        at, rest = {}, i
        for name, size in zip(reversed(AXES), reversed(SIZES)):
            at[name], rest = rest % size, rest // size
        at[axis] ^= masks[at["c"]]
        j = 0
        for name, size in zip(AXES, SIZES):
            j = j * size + at[name]
        pairs.append((i, j))
    return lax.ppermute(value, BOTH, pairs)


def swap(value):
    return exchange(value, ("c", 1, 1))


def place(info, steps, bits, core=None):
    at = {name: info[k] for k, name in enumerate(AXES)}
    core = info[4] if core is None else core
    for step, bit in zip(steps, bits):
        if bit:
            axis, first, second = step
            at[axis] = lax.bitwise_xor(at[axis], first + core * (second - first))
    return at


def params(limit):
    return pltpu.CompilerParams(vmem_limit_bytes=limit * MIB)


VMEM = pl.BlockSpec(memory_space=pltpu.VMEM)
SMEM = pl.BlockSpec(memory_space=pltpu.SMEM)
ANY = pl.BlockSpec(memory_space=pl.ANY)


def chip_slots(info, steps, core=None):
    chips = []
    for s in range(8):
        at = place(info, steps, (s >> 2 & 1, s >> 1 & 1, s & 1), core)
        chips.append(at["x"] * 2 + at["l"])
    return chips


def degree_kernel(info, index, tiles, own, other, acc, buf, sem):
    count, core = index[96], info[4]

    def begin(s, carry):
        pltpu.make_async_copy(tiles.at[s], buf.at[s], sem.at[s]).start()
        return carry

    lax.fori_loop(0, count, begin, 0)
    acc[...] = jnp.zeros_like(acc)
    ones = jnp.ones((8, buf.shape[1]), jnp.bfloat16)

    def visit(s, carry):
        pltpu.make_async_copy(tiles.at[s], buf.at[s], sem.at[s]).wait()
        acc[index[s]] += lax.dot_general(
            ones, buf[s], CONTRACT_COLS, preferred_element_type=jnp.float32
        )
        return carry

    lax.fori_loop(0, count, visit, 0)
    for s, chip in enumerate(chip_slots(info, REDUCE[0])):
        own[s] = acc[chip * 2 + core]
    for s, chip in enumerate(chip_slots(info, REDUCE[0], 1 - core)):
        other[s] = acc[chip * 2 + 1 - core]


def partial_degree(info, index, tiles):
    slots, edge, _ = tiles.shape
    return pl.pallas_call(
        degree_kernel,
        out_shape=[jax.ShapeDtypeStruct((8, 8, edge), jnp.float32)] * 2,
        in_specs=[SMEM, SMEM, ANY],
        out_specs=[VMEM] * 2,
        scratch_shapes=[
            pltpu.VMEM((16, 8, edge), jnp.float32),
            pltpu.VMEM((slots, edge, edge), jnp.bfloat16),
            pltpu.SemaphoreType.DMA((slots,)),
        ],
        compiler_params=params(16),
        name="degree",
    )(info, index, tiles)


def degree_stages(info, index, tiles):
    def begin(state):
        own, other = partial_degree(info, index, tiles)
        return own + swap(other)

    def add(total):
        for step, n in zip(REDUCE[0], (4, 2, 1)):
            total = total[:n] + exchange(total[n:], step)
        return total

    return (None, None, begin, add)


def spread_kernel(info, index0, index1, tiles0, tiles1, *refs):
    pieces, (send0, keep0, send1, keep1, x, acc, buf, sem, piece_sem) = refs[:4], refs[4:]
    core = info[4]
    slots = tiles0.shape[0]

    copies = []
    for chain, (steps, (first, rows)) in enumerate(zip(GATHER, ROWS)):
        for s in range(16):
            at = place(info, steps, (s & 1, s >> 1 & 1, s >> 2 & 1, s >> 3))
            block = at["y"] * 4 + at["z"]
            copies.append(
                pltpu.make_async_copy(
                    pieces[chain * 2 + s // 8].at[s % 8],
                    x.at[pl.ds(block * 2, 2), pl.ds(first, rows), :],
                    piece_sem.at[chain, s],
                )
            )
    for copy in copies:
        copy.start()

    def tile_copy(tiles, base, s):
        return pltpu.make_async_copy(tiles.at[s], buf.at[base + s], sem.at[base + s])

    work = ((index0, tiles0, 0), (index1, tiles1, 1))
    for index, tiles, rel in work:

        def begin(s, carry, tiles=tiles, base=rel * slots):
            tile_copy(tiles, base, s).start()
            return carry

        lax.fori_loop(0, index[96], begin, 0)
    acc[...] = jnp.zeros_like(acc)
    for copy in copies:
        copy.wait()
    for index, tiles, rel in work:

        def visit(s, carry, index=index, tiles=tiles, rel=rel):
            tile_copy(tiles, rel * slots, s).wait()
            acc[index[s]] += jnp.dot(
                buf[rel * slots + s],
                x[index[48 + s] * 2 + rel],
                preferred_element_type=jnp.float32,
            )
            return carry

        lax.fori_loop(0, index[96], visit, 0)
    for chain, (send, keep) in enumerate(((send0, keep0), (send1, keep1))):
        cols = slice(chain * 128, chain * 128 + 128)
        for s, chip in enumerate(chip_slots(info, REDUCE[chain])):
            for rel in range(2):
                block = chip * 2 + (core if rel == 0 else 1 - core)
                if s < 4:
                    keep[s, rel] = acc[block, :, cols]
                else:
                    send[s - 4, rel] = acc[block, :, cols].astype(jnp.bfloat16)


def spread(info, work, pieces):
    (index0, tiles0), (index1, tiles1) = work
    slots, edge, _ = tiles0.shape
    quarter = (4, 2, edge, 128)
    return pl.pallas_call(
        spread_kernel,
        out_shape=[
            jax.ShapeDtypeStruct(quarter, jnp.bfloat16),
            jax.ShapeDtypeStruct(quarter, jnp.float32),
        ]
        * 2,
        in_specs=[SMEM] * 3 + [ANY] * 6,
        out_specs=[VMEM] * 4,
        scratch_shapes=[
            pltpu.VMEM((32, edge, 256), jnp.bfloat16),
            pltpu.VMEM((16, edge, 256), jnp.float32),
            pltpu.VMEM((2 * slots, edge, edge), jnp.bfloat16),
            pltpu.SemaphoreType.DMA((2 * slots,)),
            pltpu.SemaphoreType.DMA((2, 16)),
        ],
        compiler_params=params(36),
        cost_estimate=pl.CostEstimate(
            flops=2 * 47 * edge * edge * 512, bytes_accessed=20 * MIB, transcendentals=0
        ),
        name="spread",
    )(info, index0, index1, tiles0, tiles1, *pieces)


def join_kernel(keep, got, send, rest):
    n = rest.shape[0]
    for s in range(2 * n):
        total = keep[s] + got[s].astype(jnp.float32)
        if s < n:
            rest[s] = total
        else:
            send[s - n] = total.astype(jnp.bfloat16)


def join(keep, got):
    shape = (keep.shape[0] // 2,) + keep.shape[1:]
    return pl.pallas_call(
        join_kernel,
        out_shape=[
            jax.ShapeDtypeStruct(shape, jnp.bfloat16),
            jax.ShapeDtypeStruct(shape, jnp.float32),
        ],
        in_specs=[VMEM] * 2,
        out_specs=[VMEM] * 2,
        compiler_params=params(16),
        name="join",
    )(keep, got)


def last_join_kernel(keep0, got0, keep1, got1, own, other):
    for chain, (keep, got) in enumerate(((keep0, got0), (keep1, got1))):
        cols = slice(chain * 128, chain * 128 + 128)
        own[:, cols] = keep[0, 0] + got[0, 0].astype(jnp.float32)
        other[:, cols] = keep[0, 1] + got[0, 1].astype(jnp.float32)


def last_join(keep0, got0, keep1, got1):
    edge = keep0.shape[2]
    return pl.pallas_call(
        last_join_kernel,
        out_shape=[jax.ShapeDtypeStruct((edge, 256), jnp.float32)] * 2,
        in_specs=[VMEM] * 4,
        out_specs=[VMEM] * 2,
        compiler_params=params(16),
        name="last_join",
    )(keep0, got0, keep1, got1)


def aggregate(info, work, own_half, other_half, stages, state):
    arrived = swap(other_half)
    pair = jnp.stack([own_half, arrived])
    have = [pair[None, :, first : first + rows] for first, rows in ROWS]
    for k in range(4):
        got = [exchange(h, steps[k]) for h, steps in zip(have, GATHER)]
        if stages[k] is not None:
            state = stages[k](state)
            got, state = lax.optimization_barrier((got, state))
        if k < 3:
            have = [jnp.concatenate([h, g]) for h, g in zip(have, got)]
            have = lax.optimization_barrier(have)
    send0, keep0, send1, keep1 = spread(info, work, (have[0], got[0], have[1], got[1]))
    send, keep = [send0, send1], [keep0, keep1]
    for k in range(2):
        arrived = [exchange(send[chain], REDUCE[chain][k]) for chain in range(2)]
        arrived = lax.optimization_barrier(arrived)
        for chain in range(2):
            send[chain], keep[chain] = join(keep[chain], arrived[chain])
    arrived = [exchange(send[chain], REDUCE[chain][2]) for chain in range(2)]
    own, other = last_join(keep[0], arrived[0], keep[1], arrived[1])
    return own, swap(other), state


def whole_width(core, own, got):
    first = core == 0
    return jnp.concatenate([jnp.where(first, own, got), jnp.where(first, got, own)], axis=1)


def dense_kernel(
    info, features, cotangent, w_self, w_neigh, degree, own, got, output, grad_pre, mean, mine, theirs
):
    deg = degree[:, 0:1]
    core = info[4]
    summed = whole_width(core, own[...], got[...])
    neighbor_mean = (summed / deg).astype(jnp.bfloat16)
    mean[...] = neighbor_mean
    preact = jnp.dot(features[...], w_self[...], preferred_element_type=jnp.float32) + jnp.dot(
        neighbor_mean, w_neigh[...], preferred_element_type=jnp.float32
    )
    part = jax.nn.sigmoid(preact)
    output[...] = (preact * part).astype(jnp.bfloat16)
    grad = (
        cotangent[...].astype(jnp.float32) * part * (1.0 + preact * (1.0 - part))
    ).astype(jnp.bfloat16)
    grad_pre[...] = grad
    back = (
        lax.dot_general(grad, w_neigh[...], CONTRACT_COLS, preferred_element_type=jnp.float32)
        / deg
    )
    mine[...] = jnp.where(core == 0, back[:, :256], back[:, 256:]).astype(jnp.bfloat16)
    theirs[...] = jnp.where(core == 0, back[:, 256:], back[:, :256]).astype(jnp.bfloat16)


def dense(info, features, cotangent, w_self, w_neigh, degree, own, got):
    nodes, width = features.shape
    full = jax.ShapeDtypeStruct((nodes, width), jnp.bfloat16)
    half = jax.ShapeDtypeStruct((nodes, 256), jnp.bfloat16)
    return pl.pallas_call(
        dense_kernel,
        out_shape=[full] * 3 + [half] * 2,
        in_specs=[SMEM] + [VMEM] * 7,
        out_specs=[VMEM] * 5,
        compiler_params=params(24),
        name="dense",
    )(info, features, cotangent, w_self, w_neigh, degree, own, got)


def weights_kernel(info, features, mean, grad_pre, w_self, keep, send, own):
    grad = grad_pre[...]
    grad_self = lax.dot_general(
        features[...], grad, CONTRACT_ROWS, preferred_element_type=jnp.float32
    )
    grad_neigh = lax.dot_general(
        mean[...], grad, CONTRACT_ROWS, preferred_element_type=jnp.float32
    )
    first = info[4] == 0
    keep[...] = jnp.where(first, grad_self, grad_neigh)
    send[...] = jnp.where(first, grad_neigh, grad_self)
    own[...] = lax.dot_general(
        grad, w_self[...], CONTRACT_COLS, preferred_element_type=jnp.float32
    )


def weights(info, features, mean, grad_pre, w_self):
    nodes, width = features.shape
    square = jax.ShapeDtypeStruct((width, width), jnp.float32)
    return pl.pallas_call(
        weights_kernel,
        out_shape=[square, square, jax.ShapeDtypeStruct((nodes, width), jnp.float32)],
        in_specs=[SMEM] + [VMEM] * 4,
        out_specs=[VMEM] * 3,
        compiler_params=params(24),
        name="weights",
    )(info, features, mean, grad_pre, w_self)


def weight_blocks_kernel(info, keep, got, send, rest):
    for s, chip in enumerate(chip_slots(info, REDUCE[0])):
        rows = pl.ds(pl.multiple_of(chip * 64, 64), 64)
        total = keep[rows, :] + got[rows, :]
        if s < 4:
            rest[s] = total
        else:
            send[s - 4] = total


def weight_blocks(info, keep, got):
    shape = jax.ShapeDtypeStruct((4, 64, keep.shape[1]), jnp.float32)
    return pl.pallas_call(
        weight_blocks_kernel,
        out_shape=[shape] * 2,
        in_specs=[SMEM, VMEM, VMEM],
        out_specs=[VMEM] * 2,
        compiler_params=params(16),
        name="weight_blocks",
    )(info, keep, got)


def weight_stages(info, features, w_self):
    steps = REDUCE[0]

    def local(state):
        grad_pre, mean = state
        keep, send, own_term = weights(info, features, mean, grad_pre, w_self)
        return keep, swap(send), own_term

    def first(state):
        keep, got, own_term = state
        send, rest = weight_blocks(info, keep, got)
        return rest + exchange(send, steps[0]), own_term

    def middle(state):
        total, own_term = state
        total = total[:2] + exchange(total[2:], steps[1])
        return total[0] + exchange(total[1], steps[2]), own_term

    def last(state):
        total, own_term = state
        for step in ROW_SUM:
            total = total + exchange(total, step)
        return total, own_term

    return (local, first, middle, last)


def split_weights(total):
    every = lax.all_gather(total, "col", axis=0, tiled=False)
    width = total.shape[1]
    both = every.reshape(8, 2, 64, width)
    return both[:, 0].reshape(-1, width), both[:, 1].reshape(-1, width)


def finish_kernel(info, own_term, own, got, out):
    out[...] = (own_term[...] + whole_width(info[4], own[...], got[...])).astype(jnp.bfloat16)


def finish(info, own_term, own, got):
    return pl.pallas_call(
        finish_kernel,
        out_shape=jax.ShapeDtypeStruct(own_term.shape, jnp.bfloat16),
        in_specs=[SMEM] + [VMEM] * 3,
        out_specs=VMEM,
        compiler_params=params(16),
        name="finish",
    )(info, own_term, own, got)


def shards(features, w_self, w_neigh, cotangent, tile_values, tile_dst, tile_src, tile_count):
    row, col = lax.axis_index("row"), lax.axis_index("col")
    core = col % 2
    info = jnp.stack([row // 4, row % 4, col // 4, col // 2 % 2, core]).astype(jnp.int32)
    index = jnp.concatenate([tile_dst, tile_src, tile_count])
    work = ((index, tile_values), (swap(index), swap(tile_values)))

    first = core == 0
    mine = jnp.where(first, features[:, :256], features[:, 256:])
    theirs = jnp.where(first, features[:, 256:], features[:, :256])
    own, got, degree = aggregate(
        info, work, mine, theirs, degree_stages(info, index, tile_values), None
    )
    degree = jnp.broadcast_to(degree[0, 0][:, None], (degree.shape[-1], 128))
    output, grad_pre, mean, mine, theirs = dense(
        info, features, cotangent, w_self, w_neigh, degree, own, got
    )
    own, got, (total, own_term) = aggregate(
        info, work, mine, theirs, weight_stages(info, features, w_self), (grad_pre, mean)
    )
    grad_self, grad_neigh = split_weights(total)
    grad_features = finish(info, own_term, own, got)
    return (output, grad_features, grad_self, grad_neigh)


def solution(mesh):
    return jax.shard_map(
        shards,
        mesh=mesh,
        in_specs=(
            P(("row", "col"), None),
            P(),
            P(),
            P(("row", "col"), None),
            P(("row", "col"), None, None),
            P(("row", "col")),
            P(("row", "col")),
            P(("row", "col")),
        ),
        out_specs=(P(("row", "col"), None), P(("row", "col"), None), P(), P()),
        check_vma=False,
    )
```

time: 739 us -> 296 us (0.40)
  waiting for transfers between devices: 521 us -> 138 us
  starting transfers between devices: 0.2 us -> 88 us
  blocking collectives: 80.9 us -> 0 us
  other arithmetic: 51.1 us -> 3.78 us
  Pallas kernels: 0 us -> 37.3 us
  local copies, waits for them, and re-layouts: 44.6 us -> 8.93 us
  matrix products: 23.2 us -> 0 us
    psum x1 -> x0, waiting for transfers between devices: 212 us -> none  [shards(): grad_self, grad_neigh = lax.psum((local_self, local_neigh), ('row', 'col'))]
    reduce_scatter x2 -> x0, waiting for transfers between devices: 190 us -> none  [the longest x1 96.3 us: shards(): lax.psum_scatter(partial_back.astype(jnp.bfloat16), 'row', scatter_dimens...]
    ppermute x0 -> x46, waiting for transfers between devices: none -> 138 us  [exchange(): return lax.ppermute(value, BOTH, pairs)]
    all_gather x2 -> x1, waiting for transfers between devices: 118 us -> 0.01 us  [split_weights(): every = lax.all_gather(total, 'col', axis=0, tiled=False)]
    ppermute x0 -> x46, starting transfers between devices: none -> 88 us  [exchange(): return lax.ppermute(value, BOTH, pairs)]
    unnamed x1 -> x0, blocking collectives: 80.9 us -> none
    pallas_call x0 -> x17, Pallas kernels: none -> 37.3 us  [the longest x2 25.2 us: spread(): pl.pallas_call(spread_kernel, out_shape=[jax.ShapeDtypeStruct(quarter, jn...]
    scatter-add x9 -> x0, other arithmetic: 34.7 us -> none  [the longest x8 33.8 us: visit(): return totals.at[targets].add(product * active[:, None, None])]
  transfers between devices with their start and end apart: 5 -> 47, of which waited for: 5 -> 31; matrix products, arithmetic and copies ran while one was open for 9% -> 1% of each run, Pallas kernels for 0% -> 7%
where the time goes in v1:
time: 296 us; the launch traced here: 292 us
  waiting for transfers between devices  138 us (47%)
  starting transfers between devices  88 us (30%)
  Pallas kernels  37.3 us (13%)
  between operations  15.2 us (5%)
  local copies, waits for them, and re-layouts  8.93 us (3%)
  other arithmetic  3.78 us (1%)
    ppermute x46, waiting for transfers between devices, exchange(): return lax.ppermute(value, BOTH, pairs)  138 us
    ppermute x46, starting transfers between devices, exchange(): return lax.ppermute(value, BOTH, pairs)  88 us
    pallas_call x2, Pallas kernels, spread(): pl.pallas_call(spread_kernel, out_shape=[jax.ShapeDtypeStruct(quarter, jn...  25.2 us
    pallas_call x1, Pallas kernels, partial_degree(): pl.pallas_call(degree_kernel, out_shape=[jax.ShapeDtypeStruct((8, 8, edge...  6.38 us
  transfers between devices with their start and end apart: 47, of which 31 were waited for; matrix products, arithmetic and copies ran while one was open for 1% of the time, Pallas kernels for 7%

profile of v1, /device:TPU:1, one launch (start us, length us, event | category | flops | bytes accessed | tf_op | source)
XLA Modules:
  0.0 291.6 jit_solution(10862103511210640830)
XLA Ops:
  11.7 8.9 %collective-permute-done = bf16[256,256]{1,0:T(8,128)(2,1)S(1)} collective-permute-done((bf16[256,256]{1,0:T(8,128)(2,1)S(1)}, bf16[256,256]{1,0:T(8,128)(2,1)S(1)}, u32[]{:S(2)}, u32[]{:S(2)}) %collective-permute-start) | collective-permute-done | bytes 131104 | tf_op jit(solution)/shard_map/ppermute | solution.py:41
  21.6 6.1 %collective-permute-start.1 = (bf16[1,2,176,256]{3,2,1,0:T(8,128)(2,1)S(1)}, bf16[1,2,176,256]{3,2,1,0:T(8,128)(2,1)S(1)}, u32[]{:S(2)}, u32[]{:S(2)}) collective-permute-start(bf16[1,2,176,256]{3,2,1,0:T(8,128)(2,1)S(1)} %fusion.3), channel_id=1, source_target_pairs={{0,16},{1,49},{2,18},{3,51},{4,20},{5,53},{6,22},{7,55},{8,24},{9,... | collective-permute-start | bytes 540680 | tf_op jit(solution)/shard_map/ppermute | solution.py:41
  27.8 4.3 %collective-permute-done.1 = bf16[1,2,176,256]{3,2,1,0:T(8,128)(2,1)S(1)} collective-permute-done((bf16[1,2,176,256]{3,2,1,0:T(8,128)(2,1)S(1)}, bf16[1,2,176,256]{3,2,1,0:T(8,128)(2,1)S(1)}, u32[]{:S(2)}, u32[]{:S(2)}) %collective-permute-start.1) | collective-permute-done | bytes 180256 | tf_op jit(solution)/shard_map/ppermute | solution.py:41
  33.9 4.5 %collective-permute-done.4 = bf16[2,2,80,256]{3,2,1,0:T(8,128)(2,1)S(1)} collective-permute-done((bf16[2,2,80,256]{3,2,1,0:T(8,128)(2,1)S(1)}, bf16[2,2,80,256]{3,2,1,0:T(8,128)(2,1)S(1)}, u32[]{:S(2)}, u32[]{:S(2)}) %collective-permute-start.4) | collective-permute-done | bytes 163872 | tf_op jit(solution)/shard_map/ppermute | solution.py:41
  38.4 4.4 %collective-permute-done.3 = bf16[2,2,176,256]{3,2,1,0:T(8,128)(2,1)S(1)} collective-permute-done((bf16[2,2,176,256]{3,2,1,0:T(8,128)(2,1)S(1)}, bf16[2,2,176,256]{3,2,1,0:T(8,128)(2,1)S(1)}, u32[]{:S(2)}, u32[]{:S(2)}) %collective-permute-start.3) | collective-permute-done | bytes 360480 | tf_op jit(solution)/shard_map/ppermute | solution.py:41
  43.8 3.8 %collective-permute-start.6 = (bf16[4,2,80,256]{3,2,1,0:T(8,128)(2,1)S(1)}, bf16[4,2,80,256]{3,2,1,0:T(8,128)(2,1)S(1)}, u32[]{:S(2)}, u32[]{:S(2)}) collective-permute-start(bf16[4,2,80,256]{3,2,1,0:T(8,128)(2,1)S(1)} %pad_maximum_fusion.8), channel_id=1, source_target_pairs={{0,16},{1,49},{2,18},{3,51},{4,20},{5,53},{6,22},{7,55},{8,24},{9,... | collective-permute-start | bytes 983048 | tf_op jit(solution)/shard_map/ppermute | solution.py:41
  51.2 6.4 %degree.1 = (f32[8,8,256]{2,1,0:T(8,128)S(1)}, f32[8,8,256]{2,1,0:T(8,128)S(1)}) custom-call(s32[5]{0:T(128)S(1)} %stack.41.info, s32[97]{0:T(128)S(1)} %pad_add_fusion.index.index0, bf16[48,256,256]{2,1,0:T(8,128)(2,1)S(1)} %copy-done), custom_call_target="tpu_custom_call" | custom-call | tf_op jit(solution)/shard_map/degree/pallas_call | solution.py:102
  62.2 4.3 %collective-permute-start.10 = (f32[4,8,256]{2,1,0:T(8,128)S(1)}, f32[4,8,256]{2,1,0:T(8,128)S(1)}, u32[]{:S(2)}, u32[]{:S(2)}) collective-permute-start(f32[4,8,256]{2,1,0:T(8,128)S(1)} %slice.64), channel_id=1, source_target_pairs={{0,4},{1,13},{2,6},{3,15},{4,0},{5,9},{6,2},{7,11},{8,12},{9,5},{1... | collective-permute-start | bytes 98312 | tf_op jit(solution)/shard_map/ppermute | solution.py:41
  71.1 4.3 %collective-permute-start.13 = (s32[97]{0:T(128)S(1)}, s32[97]{0:T(128)S(1)}, u32[]{:S(2)}, u32[]{:S(2)}) collective-permute-start(s32[97]{0:T(128)S(1)} %pad_add_fusion.index.index0), channel_id=1, source_target_pairs={{0,1},{1,0},{2,3},{3,2},{4,5},{5,4},{6,7},{7,6},{8,9},{9,8},{10,11... | collective-permute-start | bytes 1172 | tf_op jit(solution)/shard_map/ppermute | solution.py:41
  75.4 6.3 %collective-permute-done.12 = f32[1,8,256]{2,1,0:T(8,128)S(1)} collective-permute-done((f32[1,8,256]{2,1,0:T(8,128)S(1)}, f32[1,8,256]{2,1,0:T(8,128)S(1)}, u32[]{:S(2)}, u32[]{:S(2)}) %collective-permute-start.12) | collective-permute-done | bytes 8224 | tf_op jit(solution)/shard_map/ppermute | solution.py:41
  82.8 12.8 %spread.2 = (bf16[4,2,256,128]{3,2,1,0:T(8,128)(2,1)S(1)}, f32[4,2,256,128]{3,2,1,0:T(8,128)S(1)}, bf16[4,2,256,128]{3,2,1,0:T(8,128)(2,1)S(1)}, f32[4,2,256,128]{3,2,1,0:T(8,128)S(1)}) custom-call(s32[5]{0:T(128)S(1)} %stack.41.info, s32[97]{0:T(128)S(1)} %pad_add_fusion.index.index0, s32[97]{0:T(128)S(1)} %collective-permute-done.13.index1, ...), custom_call_target="tpu_custom_call" | custom-call | flops 3154116608 | bytes 20971520 | tf_op jit(solution)/shard_map/spread/pallas_call | solution.py:191
  95.6 4.5 %collective-permute-start.15 = (bf16[4,2,256,128]{3,2,1,0:T(8,128)(2,1)S(1)}, bf16[4,2,256,128]{3,2,1,0:T(8,128)(2,1)S(1)}, u32[]{:S(2)}, u32[]{:S(2)}) collective-permute-start(bf16[4,2,256,128]{3,2,1,0:T(8,128)(2,1)S(1)} %get-tuple-element.102), channel_id=1, source_target_pairs={{0,4},{1,13},{2,6},{3,15},{4,0},{5,9},{6,2},{7,11},{8,12},{9,5},{1... | collective-permute-start | bytes 1572872 | tf_op jit(solution)/shard_map/ppermute | solution.py:41
  100.2 6.6 %collective-permute-done.15.got = bf16[4,2,256,128]{3,2,1,0:T(8,128)(2,1)S(1)} collective-permute-done((bf16[4,2,256,128]{3,2,1,0:T(8,128)(2,1)S(1)}, bf16[4,2,256,128]{3,2,1,0:T(8,128)(2,1)S(1)}, u32[]{:S(2)}, u32[]{:S(2)}) %collective-permute-start.15) | collective-permute-done | bytes 524320 | tf_op jit(solution)/shard_map/ppermute | solution.py:41
  106.8 5.8 %collective-permute-done.16.got = bf16[4,2,256,128]{3,2,1,0:T(8,128)(2,1)S(1)} collective-permute-done((bf16[4,2,256,128]{3,2,1,0:T(8,128)(2,1)S(1)}, bf16[4,2,256,128]{3,2,1,0:T(8,128)(2,1)S(1)}, u32[]{:S(2)}, u32[]{:S(2)}) %collective-permute-start.16) | collective-permute-done | bytes 524320 | tf_op jit(solution)/shard_map/ppermute | solution.py:41
  113.2 8.9 %collective-permute-done.18.got = bf16[2,2,256,128]{3,2,1,0:T(8,128)(2,1)S(1)} collective-permute-done((bf16[2,2,256,128]{3,2,1,0:T(8,128)(2,1)S(1)}, bf16[2,2,256,128]{3,2,1,0:T(8,128)(2,1)S(1)}, u32[]{:S(2)}, u32[]{:S(2)}) %collective-permute-start.18) | collective-permute-done | bytes 262176 | tf_op jit(solution)/shard_map/ppermute | solution.py:41
  122.5 3.6 %collective-permute-done.20.got1 = bf16[1,2,256,128]{3,2,1,0:T(8,128)(2,1)S(1)} collective-permute-done((bf16[1,2,256,128]{3,2,1,0:T(8,128)(2,1)S(1)}, bf16[1,2,256,128]{3,2,1,0:T(8,128)(2,1)S(1)}, u32[]{:S(2)}, u32[]{:S(2)}) %collective-permute-start.20) | collective-permute-done | bytes 131104 | tf_op jit(solution)/shard_map/ppermute | solution.py:41
  126.3 4.0 %collective-permute-start.21 = (f32[256,256]{1,0:T(8,128)S(1)}, f32[256,256]{1,0:T(8,128)S(1)}, u32[]{:S(2)}, u32[]{:S(2)}) collective-permute-start(f32[256,256]{1,0:T(8,128)S(1)} %get-tuple-element.118), channel_id=1, source_target_pairs={{0,1},{1,0},{2,3},{3,2},{4,5},{5,4},{6,7},{7,6},{8,9},{9,8},{10,11... | collective-permute-start | bytes 786440 | tf_op jit(solution)/shard_map/ppermute | solution.py:41
  140.1 3.6 %collective-permute-start.24 = (bf16[1,2,80,256]{3,2,1,0:T(8,128)(2,1)S(1)}, bf16[1,2,80,256]{3,2,1,0:T(8,128)(2,1)S(1)}, u32[]{:S(2)}, u32[]{:S(2)}) collective-permute-start(bf16[1,2,80,256]{3,2,1,0:T(8,128)(2,1)S(1)} %fusion.5), channel_id=1, source_target_pairs={{0,64},{1,193},{2,66},{3,195},{4,68},{5,197},{6,70},{7,199},{8,72}... | collective-permute-start | bytes 245768 | tf_op jit(solution)/shard_map/ppermute | solution.py:41
  148.4 12.3 %collective-permute-start.27 = (bf16[2,2,80,256]{3,2,1,0:T(8,128)(2,1)S(1)}, bf16[2,2,80,256]{3,2,1,0:T(8,128)(2,1)S(1)}, u32[]{:S(2)}, u32[]{:S(2)}) collective-permute-start(bf16[2,2,80,256]{3,2,1,0:T(8,128)(2,1)S(1)} %pad_maximum_fusion.11), channel_id=1, source_target_pairs={{0,192},{1,65},{2,194},{3,67},{4,196},{5,69},{6,198},{7,71},{8,200... | collective-permute-start | bytes 491528 | tf_op jit(solution)/shard_map/ppermute | solution.py:41
  173.9 9.6 %collective-permute-done.30 = bf16[4,2,80,256]{3,2,1,0:T(8,128)(2,1)S(1)} collective-permute-done((bf16[4,2,80,256]{3,2,1,0:T(8,128)(2,1)S(1)}, bf16[4,2,80,256]{3,2,1,0:T(8,128)(2,1)S(1)}, u32[]{:S(2)}, u32[]{:S(2)}) %collective-permute-start.30) | collective-permute-done | bytes 327712 | tf_op jit(solution)/shard_map/ppermute | solution.py:41
  183.7 5.9 %collective-permute-start.33 = (bf16[8,2,176,256]{3,2,1,0:T(8,128)(2,1)S(1)}, bf16[8,2,176,256]{3,2,1,0:T(8,128)(2,1)S(1)}, u32[]{:S(2)}, u32[]{:S(2)}) collective-permute-start(bf16[8,2,176,256]{3,2,1,0:T(8,128)(2,1)S(1)} %pad_maximum_fusion.1.refs_0_), channel_id=1, source_target_pairs={{0,192},{1,65},{2,194},{3,67},{4,196},{5,69},{6,198},{7,71},{8,200... | collective-permute-start | bytes 4325384 | tf_op jit(solution)/shard_map/ppermute | solution.py:41
  190.5 4.9 %collective-permute-start.35 = (f32[64,512]{1,0:T(8,128)S(1)}, f32[64,512]{1,0:T(8,128)S(1)}, u32[]{:S(2)}, u32[]{:S(2)}) collective-permute-start(f32[64,512]{1,0:T(8,128)S(1)} %fusion.4), channel_id=1, source_target_pairs={{0,64},{1,193},{2,66},{3,195},{4,68},{5,197},{6,70},{7,199},{8,72}... | collective-permute-start | bytes 393224 | tf_op jit(solution)/shard_map/ppermute | solution.py:41
  195.3 4.2 %collective-permute-done.35 = f32[64,512]{1,0:T(8,128)S(1)} collective-permute-done((f32[64,512]{1,0:T(8,128)S(1)}, f32[64,512]{1,0:T(8,128)S(1)}, u32[]{:S(2)}, u32[]{:S(2)}) %collective-permute-start.35) | collective-permute-done | bytes 131104 | tf_op jit(solution)/shard_map/ppermute | solution.py:41
  199.9 9.3 %collective-permute-done.36 = f32[64,512]{1,0:T(8,128)S(1)} collective-permute-done((f32[64,512]{1,0:T(8,128)S(1)}, f32[64,512]{1,0:T(8,128)S(1)}, u32[]{:S(2)}, u32[]{:S(2)}) %collective-permute-start.36) | collective-permute-done | bytes 131104 | tf_op jit(solution)/shard_map/ppermute | solution.py:41
  209.4 7.3 %collective-permute-done.37 = f32[64,512]{1,0:T(8,128)S(1)} collective-permute-done((f32[64,512]{1,0:T(8,128)S(1)}, f32[64,512]{1,0:T(8,128)S(1)}, u32[]{:S(2)}, u32[]{:S(2)}) %collective-permute-start.37) | collective-permute-done | bytes 131104 | tf_op jit(solution)/shard_map/ppermute | solution.py:41
  216.9 6.0 %collective-permute-done.38 = f32[64,512]{1,0:T(8,128)S(1)} collective-permute-done((f32[64,512]{1,0:T(8,128)S(1)}, f32[64,512]{1,0:T(8,128)S(1)}, u32[]{:S(2)}, u32[]{:S(2)}) %collective-permute-start.38) | collective-permute-done | bytes 131104 | tf_op jit(solution)/shard_map/ppermute | solution.py:41
  226.4 12.4 %spread.3 = (bf16[4,2,256,128]{3,2,1,0:T(8,128)(2,1)S(1)}, f32[4,2,256,128]{3,2,1,0:T(8,128)S(1)}, bf16[4,2,256,128]{3,2,1,0:T(8,128)(2,1)S(1)}, f32[4,2,256,128]{3,2,1,0:T(8,128)S(1)}) custom-call(s32[5]{0:T(128)S(1)} %stack.41.info, s32[97]{0:T(128)S(1)} %pad_add_fusion.index.index0, s32[97]{0:T(128)S(1)} %collective-permute-done.13.index1, ...), custom_call_target="tpu_custom_call" | custom-call | flops 3154116608 | bytes 20971520 | tf_op jit(solution)/shard_map/spread/pallas_call | solution.py:191
  241.7 6.6 %collective-permute-done.39.got = bf16[4,2,256,128]{3,2,1,0:T(8,128)(2,1)S(1)} collective-permute-done((bf16[4,2,256,128]{3,2,1,0:T(8,128)(2,1)S(1)}, bf16[4,2,256,128]{3,2,1,0:T(8,128)(2,1)S(1)}, u32[]{:S(2)}, u32[]{:S(2)}) %collective-permute-start.39) | collective-permute-done | bytes 524320 | tf_op jit(solution)/shard_map/ppermute | solution.py:41
  248.2 9.1 %collective-permute-done.40.got = bf16[4,2,256,128]{3,2,1,0:T(8,128)(2,1)S(1)} collective-permute-done((bf16[4,2,256,128]{3,2,1,0:T(8,128)(2,1)S(1)}, bf16[4,2,256,128]{3,2,1,0:T(8,128)(2,1)S(1)}, u32[]{:S(2)}, u32[]{:S(2)}) %collective-permute-start.40) | collective-permute-done | bytes 524320 | tf_op jit(solution)/shard_map/ppermute | solution.py:41
  257.7 6.2 %collective-permute-done.42.got = bf16[2,2,256,128]{3,2,1,0:T(8,128)(2,1)S(1)} collective-permute-done((bf16[2,2,256,128]{3,2,1,0:T(8,128)(2,1)S(1)}, bf16[2,2,256,128]{3,2,1,0:T(8,128)(2,1)S(1)}, u32[]{:S(2)}, u32[]{:S(2)}) %collective-permute-start.42) | collective-permute-done | bytes 262176 | tf_op jit(solution)/shard_map/ppermute | solution.py:41
  266.9 4.7 %collective-permute-done.44.got1 = bf16[1,2,256,128]{3,2,1,0:T(8,128)(2,1)S(1)} collective-permute-done((bf16[1,2,256,128]{3,2,1,0:T(8,128)(2,1)S(1)}, bf16[1,2,256,128]{3,2,1,0:T(8,128)(2,1)S(1)}, u32[]{:S(2)}, u32[]{:S(2)}) %collective-permute-start.44) | collective-permute-done | bytes 131104 | tf_op jit(solution)/shard_map/ppermute | solution.py:41
  271.6 7.6 %collective-permute-start.45 = (f32[256,256]{1,0:T(8,128)S(1)}, f32[256,256]{1,0:T(8,128)S(1)}, u32[]{:S(2)}, u32[]{:S(2)}) collective-permute-start(f32[256,256]{1,0:T(8,128)S(1)} %get-tuple-element.168), channel_id=1, source_target_pairs={{0,1},{1,0},{2,3},{3,2},{4,5},{5,4},{6,7},{7,6},{8,9},{9,8},{10,11... | collective-permute-start | bytes 786440 | tf_op jit(solution)/shard_map/ppermute | solution.py:41
  (143 shorter events, 67.4 us)
Async XLA Ops:
  7.2 274.5 %all-gather.3.cloned.1.call-start = ((), (), s32[]{:S(2)}) async-start(), calls=%async_computation | async-start | bytes 2228224 | tf_op jit(solution)/shard_map/all_gather | solution.py:406
  7.2 75.6 %collective-permute-start.14 = (bf16[48,256,256]{2,1,0:T(8,128)(2,1)}, bf16[48,256,256]{2,1,0:T(8,128)(2,1)}, u32[]{:S(2)}, u32[]{:S(2)}) collective-permute-start(bf16[48,256,256]{2,1,0:T(8,128)(2,1)} %tiles0.3), channel_id=1, source_target_pairs={{0,1},{1,0},{2,3},{3,2},{4,5},{5,4},{6,7},{7,6},{8,9},{9,8},{10,11... | collective-permute-start | bytes 18874376 | tf_op jit(solution)/shard_map/ppermute | solution.py:41
  11.5 9.0 %collective-permute-start = (bf16[256,256]{1,0:T(8,128)(2,1)S(1)}, bf16[256,256]{1,0:T(8,128)(2,1)S(1)}, u32[]{:S(2)}, u32[]{:S(2)}) collective-permute-start(bf16[256,256]{1,0:T(8,128)(2,1)S(1)} %get-tuple-element.172), channel_id=1, source_target_pairs={{0,1},{1,0},{2,3},{3,2},{4,5},{5,4},{6,7},{7,6},{8,9},{9,8},{10,11... | collective-permute-start | bytes 393224 | tf_op jit(solution)/shard_map/ppermute | solution.py:41
  20.5 7.2 %collective-permute-start.2 = (bf16[1,2,80,256]{3,2,1,0:T(8,128)(2,1)S(1)}, bf16[1,2,80,256]{3,2,1,0:T(8,128)(2,1)S(1)}, u32[]{:S(2)}, u32[]{:S(2)}) collective-permute-start(bf16[1,2,80,256]{3,2,1,0:T(8,128)(2,1)S(1)} %fusion.6), channel_id=1, source_target_pairs={{0,64},{1,193},{2,66},{3,195},{4,68},{5,197},{6,70},{7,199},{8,72}... | collective-permute-start | bytes 245768 | tf_op jit(solution)/shard_map/ppermute | solution.py:41
  21.6 10.5 %collective-permute-start.1 = (bf16[1,2,176,256]{3,2,1,0:T(8,128)(2,1)S(1)}, bf16[1,2,176,256]{3,2,1,0:T(8,128)(2,1)S(1)}, u32[]{:S(2)}, u32[]{:S(2)}) collective-permute-start(bf16[1,2,176,256]{3,2,1,0:T(8,128)(2,1)S(1)} %fusion.3), channel_id=1, source_target_pairs={{0,16},{1,49},{2,18},{3,51},{4,20},{5,53},{6,22},{7,55},{8,24},{9,... | collective-permute-start | bytes 540680 | tf_op jit(solution)/shard_map/ppermute | solution.py:41
  32.1 10.6 %collective-permute-start.3 = (bf16[2,2,176,256]{3,2,1,0:T(8,128)(2,1)S(1)}, bf16[2,2,176,256]{3,2,1,0:T(8,128)(2,1)S(1)}, u32[]{:S(2)}, u32[]{:S(2)}) collective-permute-start(bf16[2,2,176,256]{3,2,1,0:T(8,128)(2,1)S(1)} %pad_maximum_fusion.6), channel_id=1, source_target_pairs={{0,48},{1,17},{2,50},{3,19},{4,52},{5,21},{6,54},{7,23},{8,56},{9,... | collective-permute-start | bytes 1081352 | tf_op jit(solution)/shard_map/ppermute | solution.py:41
  42.8 16.1 %collective-permute-start.5 = (bf16[4,2,176,256]{3,2,1,0:T(8,128)(2,1)S(1)}, bf16[4,2,176,256]{3,2,1,0:T(8,128)(2,1)}, u32[]{:S(2)}, u32[]{:S(2)}) collective-permute-start(bf16[4,2,176,256]{3,2,1,0:T(8,128)(2,1)S(1)} %pad_maximum_fusion.2), channel_id=1, source_target_pairs={{0,64},{1,193},{2,66},{3,195},{4,68},{5,197},{6,70},{7,199},{8,72}... | collective-permute-start | bytes 2162696 | tf_op jit(solution)/shard_map/ppermute | solution.py:41
  43.8 15.1 %collective-permute-start.6 = (bf16[4,2,80,256]{3,2,1,0:T(8,128)(2,1)S(1)}, bf16[4,2,80,256]{3,2,1,0:T(8,128)(2,1)S(1)}, u32[]{:S(2)}, u32[]{:S(2)}) collective-permute-start(bf16[4,2,80,256]{3,2,1,0:T(8,128)(2,1)S(1)} %pad_maximum_fusion.8), channel_id=1, source_target_pairs={{0,16},{1,49},{2,18},{3,51},{4,20},{5,53},{6,22},{7,55},{8,24},{9,... | collective-permute-start | bytes 983048 | tf_op jit(solution)/shard_map/ppermute | solution.py:41
  60.2 22.5 %collective-permute-start.8 = (bf16[8,2,176,256]{3,2,1,0:T(8,128)(2,1)S(1)}, bf16[8,2,176,256]{3,2,1,0:T(8,128)(2,1)S(1)}, u32[]{:S(2)}, u32[]{:S(2)}) collective-permute-start(bf16[8,2,176,256]{3,2,1,0:T(8,128)(2,1)S(1)} %pad_maximum_fusion.refs_0_), channel_id=1, source_target_pairs={{0,192},{1,65},{2,194},{3,67},{4,196},{5,69},{6,198},{7,71},{8,200... | collective-permute-start | bytes 4325384 | tf_op jit(solution)/shard_map/ppermute | solution.py:41
  66.5 16.3 %collective-permute-start.9 = (bf16[8,2,80,256]{3,2,1,0:T(8,128)(2,1)S(1)}, bf16[8,2,80,256]{3,2,1,0:T(8,128)(2,1)S(1)}, u32[]{:S(2)}, u32[]{:S(2)}) collective-permute-start(bf16[8,2,80,256]{3,2,1,0:T(8,128)(2,1)S(1)} %pad_maximum_fusion.4.refs_2_), channel_id=1, source_target_pairs={{0,48},{1,17},{2,50},{3,19},{4,52},{5,21},{6,54},{7,23},{8,56},{9,... | collective-permute-start | bytes 1966088 | tf_op jit(solution)/shard_map/ppermute | solution.py:41
  71.1 10.7 %collective-permute-start.12 = (f32[1,8,256]{2,1,0:T(8,128)S(1)}, f32[1,8,256]{2,1,0:T(8,128)S(1)}, u32[]{:S(2)}, u32[]{:S(2)}) collective-permute-start(f32[1,8,256]{2,1,0:T(8,128)S(1)} %slice.83), channel_id=1, source_target_pairs={{0,2},{1,3},{2,0},{3,1},{4,6},{5,7},{6,4},{7,5},{8,10},{9,11},{10,... | collective-permute-start | bytes 24584 | tf_op jit(solution)/shard_map/ppermute | solution.py:41
  71.1 11.7 %collective-permute-start.13 = (s32[97]{0:T(128)S(1)}, s32[97]{0:T(128)S(1)}, u32[]{:S(2)}, u32[]{:S(2)}) collective-permute-start(s32[97]{0:T(128)S(1)} %pad_add_fusion.index.index0), channel_id=1, source_target_pairs={{0,1},{1,0},{2,3},{3,2},{4,5},{5,4},{6,7},{7,6},{8,9},{9,8},{10,11... | collective-permute-start | bytes 1172 | tf_op jit(solution)/shard_map/ppermute | solution.py:41
  95.6 11.1 %collective-permute-start.15 = (bf16[4,2,256,128]{3,2,1,0:T(8,128)(2,1)S(1)}, bf16[4,2,256,128]{3,2,1,0:T(8,128)(2,1)S(1)}, u32[]{:S(2)}, u32[]{:S(2)}) collective-permute-start(bf16[4,2,256,128]{3,2,1,0:T(8,128)(2,1)S(1)} %get-tuple-element.102), channel_id=1, source_target_pairs={{0,4},{1,13},{2,6},{3,15},{4,0},{5,9},{6,2},{7,11},{8,12},{9,5},{1... | collective-permute-start | bytes 1572872 | tf_op jit(solution)/shard_map/ppermute | solution.py:41
  100.2 12.4 %collective-permute-start.16 = (bf16[4,2,256,128]{3,2,1,0:T(8,128)(2,1)S(1)}, bf16[4,2,256,128]{3,2,1,0:T(8,128)(2,1)S(1)}, u32[]{:S(2)}, u32[]{:S(2)}) collective-permute-start(bf16[4,2,256,128]{3,2,1,0:T(8,128)(2,1)S(1)} %get-tuple-element.103), channel_id=1, source_target_pairs={{0,2},{1,3},{2,0},{3,1},{4,6},{5,7},{6,4},{7,5},{8,10},{9,11},{10,... | collective-permute-start | bytes 1572872 | tf_op jit(solution)/shard_map/ppermute | solution.py:41
  112.7 9.4 %collective-permute-start.18 = (bf16[2,2,256,128]{3,2,1,0:T(8,128)(2,1)S(1)}, bf16[2,2,256,128]{3,2,1,0:T(8,128)(2,1)S(1)}, u32[]{:S(2)}, u32[]{:S(2)}) collective-permute-start(bf16[2,2,256,128]{3,2,1,0:T(8,128)(2,1)S(1)} %get-tuple-element.109), channel_id=1, source_target_pairs={{0,4},{1,13},{2,6},{3,15},{4,0},{5,9},{6,2},{7,11},{8,12},{9,5},{1... | collective-permute-start | bytes 786440 | tf_op jit(solution)/shard_map/ppermute | solution.py:41
  113.1 9.0 %collective-permute-start.17 = (bf16[2,2,256,128]{3,2,1,0:T(8,128)(2,1)S(1)}, bf16[2,2,256,128]{3,2,1,0:T(8,128)(2,1)S(1)}, u32[]{:S(2)}, u32[]{:S(2)}) collective-permute-start(bf16[2,2,256,128]{3,2,1,0:T(8,128)(2,1)S(1)} %get-tuple-element.106), channel_id=1, source_target_pairs={{0,12},{1,5},{2,14},{3,7},{4,8},{5,1},{6,10},{7,3},{8,4},{9,13},{1... | collective-permute-start | bytes 786440 | tf_op jit(solution)/shard_map/ppermute | solution.py:41
  134.6 10.9 %collective-permute-start.25 = (f32[512,512]{1,0:T(8,128)S(1)}, f32[512,512]{1,0:T(8,128)S(1)}, u32[]{:S(2)}, u32[]{:S(2)}) collective-permute-start(f32[512,512]{1,0:T(8,128)S(1)} %get-tuple-element.125), channel_id=1, source_target_pairs={{0,1},{1,0},{2,3},{3,2},{4,5},{5,4},{6,7},{7,6},{8,9},{9,8},{10,11... | collective-permute-start | bytes 3145736 | tf_op jit(solution)/shard_map/ppermute | solution.py:41
  137.6 8.0 %collective-permute-start.23 = (bf16[1,2,176,256]{3,2,1,0:T(8,128)(2,1)S(1)}, bf16[1,2,176,256]{3,2,1,0:T(8,128)(2,1)S(1)}, u32[]{:S(2)}, u32[]{:S(2)}) collective-permute-start(bf16[1,2,176,256]{3,2,1,0:T(8,128)(2,1)S(1)} %fusion.1), channel_id=1, source_target_pairs={{0,16},{1,49},{2,18},{3,51},{4,20},{5,53},{6,22},{7,55},{8,24},{9,... | collective-permute-start | bytes 540680 | tf_op jit(solution)/shard_map/ppermute | solution.py:41
  146.2 14.4 %collective-permute-start.28 = (f32[4,64,512]{2,1,0:T(8,128)S(1)}, f32[4,64,512]{2,1,0:T(8,128)S(1)}, u32[]{:S(2)}, u32[]{:S(2)}) collective-permute-start(f32[4,64,512]{2,1,0:T(8,128)S(1)} %get-tuple-element.134), channel_id=1, source_target_pairs={{0,4},{1,13},{2,6},{3,15},{4,0},{5,9},{6,2},{7,11},{8,12},{9,5},{1... | collective-permute-start | bytes 1572872 | tf_op jit(solution)/shard_map/ppermute | solution.py:41
  148.3 15.4 %collective-permute-start.26 = (bf16[2,2,176,256]{3,2,1,0:T(8,128)(2,1)S(1)}, bf16[2,2,176,256]{3,2,1,0:T(8,128)(2,1)S(1)}, u32[]{:S(2)}, u32[]{:S(2)}) collective-permute-start(bf16[2,2,176,256]{3,2,1,0:T(8,128)(2,1)S(1)} %pad_maximum_fusion.7), channel_id=1, source_target_pairs={{0,48},{1,17},{2,50},{3,19},{4,52},{5,21},{6,54},{7,23},{8,56},{9,... | collective-permute-start | bytes 1081352 | tf_op jit(solution)/shard_map/ppermute | solution.py:41
  148.4 15.3 %collective-permute-start.27 = (bf16[2,2,80,256]{3,2,1,0:T(8,128)(2,1)S(1)}, bf16[2,2,80,256]{3,2,1,0:T(8,128)(2,1)S(1)}, u32[]{:S(2)}, u32[]{:S(2)}) collective-permute-start(bf16[2,2,80,256]{3,2,1,0:T(8,128)(2,1)S(1)} %pad_maximum_fusion.11), channel_id=1, source_target_pairs={{0,192},{1,65},{2,194},{3,67},{4,196},{5,69},{6,198},{7,71},{8,200... | collective-permute-start | bytes 491528 | tf_op jit(solution)/shard_map/ppermute | solution.py:41
  163.9 19.6 %collective-permute-start.29 = (bf16[4,2,176,256]{3,2,1,0:T(8,128)(2,1)S(1)}, bf16[4,2,176,256]{3,2,1,0:T(8,128)(2,1)S(1)}, u32[]{:S(2)}, u32[]{:S(2)}) collective-permute-start(bf16[4,2,176,256]{3,2,1,0:T(8,128)(2,1)S(1)} %pad_maximum_fusion.3), channel_id=1, source_target_pairs={{0,64},{1,193},{2,66},{3,195},{4,68},{5,197},{6,70},{7,199},{8,72}... | collective-permute-start | bytes 2162696 | tf_op jit(solution)/shard_map/ppermute | solution.py:41
  171.2 12.3 %collective-permute-start.30 = (bf16[4,2,80,256]{3,2,1,0:T(8,128)(2,1)S(1)}, bf16[4,2,80,256]{3,2,1,0:T(8,128)(2,1)S(1)}, u32[]{:S(2)}, u32[]{:S(2)}) collective-permute-start(bf16[4,2,80,256]{3,2,1,0:T(8,128)(2,1)S(1)} %pad_maximum_fusion.9), channel_id=1, source_target_pairs={{0,16},{1,49},{2,18},{3,51},{4,20},{5,53},{6,22},{7,55},{8,24},{9,... | collective-permute-start | bytes 983048 | tf_op jit(solution)/shard_map/ppermute | solution.py:41
  183.7 39.9 %collective-permute-start.33 = (bf16[8,2,176,256]{3,2,1,0:T(8,128)(2,1)S(1)}, bf16[8,2,176,256]{3,2,1,0:T(8,128)(2,1)S(1)}, u32[]{:S(2)}, u32[]{:S(2)}) collective-permute-start(bf16[8,2,176,256]{3,2,1,0:T(8,128)(2,1)S(1)} %pad_maximum_fusion.1.refs_0_), channel_id=1, source_target_pairs={{0,192},{1,65},{2,194},{3,67},{4,196},{5,69},{6,198},{7,71},{8,200... | collective-permute-start | bytes 4325384 | tf_op jit(solution)/shard_map/ppermute | solution.py:41
  189.6 34.0 %collective-permute-start.34 = (bf16[8,2,80,256]{3,2,1,0:T(8,128)(2,1)S(1)}, bf16[8,2,80,256]{3,2,1,0:T(8,128)(2,1)}, u32[]{:S(2)}, u32[]{:S(2)}) collective-permute-start(bf16[8,2,80,256]{3,2,1,0:T(8,128)(2,1)S(1)} %pad_maximum_fusion.5.refs_2_), channel_id=1, source_target_pairs={{0,48},{1,17},{2,50},{3,19},{4,52},{5,21},{6,54},{7,23},{8,56},{9,... | collective-permute-start | bytes 1966088 | tf_op jit(solution)/shard_map/ppermute | solution.py:41
  190.5 9.1 %collective-permute-start.35 = (f32[64,512]{1,0:T(8,128)S(1)}, f32[64,512]{1,0:T(8,128)S(1)}, u32[]{:S(2)}, u32[]{:S(2)}) collective-permute-start(f32[64,512]{1,0:T(8,128)S(1)} %fusion.4), channel_id=1, source_target_pairs={{0,64},{1,193},{2,66},{3,195},{4,68},{5,197},{6,70},{7,199},{8,72}... | collective-permute-start | bytes 393224 | tf_op jit(solution)/shard_map/ppermute | solution.py:41
  199.6 9.6 %collective-permute-start.36 = (f32[64,512]{1,0:T(8,128)S(1)}, f32[64,512]{1,0:T(8,128)S(1)}, u32[]{:S(2)}, u32[]{:S(2)}) collective-permute-start(f32[64,512]{1,0:T(8,128)S(1)} %add.56), channel_id=1, source_target_pairs={{0,192},{1,65},{2,194},{3,67},{4,196},{5,69},{6,198},{7,71},{8,200... | collective-permute-start | bytes 393224 | tf_op jit(solution)/shard_map/ppermute | solution.py:41
  209.2 7.4 %collective-permute-start.37 = (f32[64,512]{1,0:T(8,128)S(1)}, f32[64,512]{1,0:T(8,128)S(1)}, u32[]{:S(2)}, u32[]{:S(2)}) collective-permute-start(f32[64,512]{1,0:T(8,128)S(1)} %add.57), channel_id=1, source_target_pairs={{0,16},{1,49},{2,18},{3,51},{4,20},{5,53},{6,22},{7,55},{8,24},{9,... | collective-permute-start | bytes 393224 | tf_op jit(solution)/shard_map/ppermute | solution.py:41
  238.8 9.5 %collective-permute-start.39 = (bf16[4,2,256,128]{3,2,1,0:T(8,128)(2,1)S(1)}, bf16[4,2,256,128]{3,2,1,0:T(8,128)(2,1)S(1)}, u32[]{:S(2)}, u32[]{:S(2)}) collective-permute-start(bf16[4,2,256,128]{3,2,1,0:T(8,128)(2,1)S(1)} %get-tuple-element.152), channel_id=1, source_target_pairs={{0,4},{1,13},{2,6},{3,15},{4,0},{5,9},{6,2},{7,11},{8,12},{9,5},{1... | collective-permute-start | bytes 1572872 | tf_op jit(solution)/shard_map/ppermute | solution.py:41
  241.7 15.6 %collective-permute-start.40 = (bf16[4,2,256,128]{3,2,1,0:T(8,128)(2,1)S(1)}, bf16[4,2,256,128]{3,2,1,0:T(8,128)(2,1)S(1)}, u32[]{:S(2)}, u32[]{:S(2)}) collective-permute-start(bf16[4,2,256,128]{3,2,1,0:T(8,128)(2,1)S(1)} %get-tuple-element.153), channel_id=1, source_target_pairs={{0,2},{1,3},{2,0},{3,1},{4,6},{5,7},{6,4},{7,5},{8,10},{9,11},{10,... | collective-permute-start | bytes 1572872 | tf_op jit(solution)/shard_map/ppermute | solution.py:41
  257.6 7.5 %collective-permute-start.41 = (bf16[2,2,256,128]{3,2,1,0:T(8,128)(2,1)S(1)}, bf16[2,2,256,128]{3,2,1,0:T(8,128)(2,1)S(1)}, u32[]{:S(2)}, u32[]{:S(2)}) collective-permute-start(bf16[2,2,256,128]{3,2,1,0:T(8,128)(2,1)S(1)} %get-tuple-element.156), channel_id=1, source_target_pairs={{0,12},{1,5},{2,14},{3,7},{4,8},{5,1},{6,10},{7,3},{8,4},{9,13},{1... | collective-permute-start | bytes 786440 | tf_op jit(solution)/shard_map/ppermute | solution.py:41
  271.6 8.7 %collective-permute-start.45 = (f32[256,256]{1,0:T(8,128)S(1)}, f32[256,256]{1,0:T(8,128)S(1)}, u32[]{:S(2)}, u32[]{:S(2)}) collective-permute-start(f32[256,256]{1,0:T(8,128)S(1)} %get-tuple-element.168), channel_id=1, source_target_pairs={{0,1},{1,0},{2,3},{3,2},{4,5},{5,4},{6,7},{7,6},{8,9},{9,8},{10,11... | collective-permute-start | bytes 786440 | tf_op jit(solution)/shard_map/ppermute | solution.py:41
  (27 other events, 318.6 us)
Sparse Core Ops, SparseCore 0:
  223.7 48.6 all-gather.2

commit v2 on v1

--- a/solution.py
+++ b/solution.py
@@ -8,6 +8,7 @@
 from jax.sharding import PartitionSpec as P
 
 MIB = 1 << 20
+UNROLL = 4
 BOTH = ("row", "col")
 CONTRACT_ROWS = (((0,), (0,)), ((), ()))
 CONTRACT_COLS = (((1,), (1,)), ((), ()))
@@ -72,42 +73,46 @@
     return chips
 
 
-def degree_kernel(info, index, tiles, own, other, acc, buf, sem):
+def degree_kernel(info, index, tiles, own, other, acc):
     count, core = index[96], info[4]
-
-    def begin(s, carry):
-        pltpu.make_async_copy(tiles.at[s], buf.at[s], sem.at[s]).start()
+    acc[...] = jnp.zeros_like(acc)
+
+    def add(s):
+        values = tiles[s].astype(jnp.float32)
+        acc[index[s]] += values[:, :128] + values[:, 128:]
+
+    def several(group, carry):
+        for k in range(UNROLL):
+            add(group * UNROLL + k)
         return carry
 
-    lax.fori_loop(0, count, begin, 0)
-    acc[...] = jnp.zeros_like(acc)
-    ones = jnp.ones((8, buf.shape[1]), jnp.bfloat16)
-
-    def visit(s, carry):
-        pltpu.make_async_copy(tiles.at[s], buf.at[s], sem.at[s]).wait()
-        acc[index[s]] += lax.dot_general(
-            ones, buf[s], CONTRACT_COLS, preferred_element_type=jnp.float32
-        )
+    def single(s, carry):
+        add(s)
         return carry
 
-    lax.fori_loop(0, count, visit, 0)
+    groups = lax.div(count, UNROLL)
+    lax.fori_loop(0, groups, several, 0)
+    lax.fori_loop(groups * UNROLL, count, single, 0)
+
+    def sums(block):
+        total = jnp.sum(jnp.transpose(acc[block]), axis=0, keepdims=True)
+        return jnp.broadcast_to(total, (8, total.shape[1]))
+
     for s, chip in enumerate(chip_slots(info, REDUCE[0])):
-        own[s] = acc[chip * 2 + core]
+        own[s] = sums(chip * 2 + core)
     for s, chip in enumerate(chip_slots(info, REDUCE[0], 1 - core)):
-        other[s] = acc[chip * 2 + 1 - core]
+        other[s] = sums(chip * 2 + 1 - core)
 
 
 def partial_degree(info, index, tiles):
-    slots, edge, _ = tiles.shape
+    edge = tiles.shape[1]
     return pl.pallas_call(
         degree_kernel,
         out_shape=[jax.ShapeDtypeStruct((8, 8, edge), jnp.float32)] * 2,
-        in_specs=[SMEM, SMEM, ANY],
+        in_specs=[SMEM, SMEM, VMEM],
         out_specs=[VMEM] * 2,
         scratch_shapes=[
-            pltpu.VMEM((16, 8, edge), jnp.float32),
-            pltpu.VMEM((slots, edge, edge), jnp.bfloat16),
-            pltpu.SemaphoreType.DMA((slots,)),
+            pltpu.VMEM((16, edge, 128), jnp.float32),
         ],
         compiler_params=params(16),
         name="degree",
@@ -119,12 +124,17 @@
         own, other = partial_degree(info, index, tiles)
         return own + swap(other)
 
-    def add(total):
-        for step, n in zip(REDUCE[0], (4, 2, 1)):
+    def add(total, part):
+        for step, n in part:
             total = total[:n] + exchange(total[n:], step)
         return total
 
-    return (None, None, begin, add)
+    parts = list(zip(REDUCE[0], (4, 2, 1)))
+    return {
+        1: begin,
+        2: lambda total: add(total, parts[:2]),
+        3: lambda total: add(total, parts[2:]),
+    }
 
 
 def spread_kernel(info, index0, index1, tiles0, tiles1, *refs):
@@ -163,38 +173,49 @@
         copy.wait()
     for index, tiles, rel in work:
 
-        def visit(s, carry, index=index, tiles=tiles, rel=rel):
-            tile_copy(tiles, rel * slots, s).wait()
+        def multiply(s, index=index, rel=rel):
             acc[index[s]] += jnp.dot(
                 buf[rel * slots + s],
                 x[index[48 + s] * 2 + rel],
                 preferred_element_type=jnp.float32,
             )
+
+        def several(group, carry, tiles=tiles, rel=rel, multiply=multiply):
+            for k in range(UNROLL):
+                tile_copy(tiles, rel * slots, group * UNROLL + k).wait()
+            for k in range(UNROLL):
+                multiply(group * UNROLL + k)
             return carry
 
-        lax.fori_loop(0, index[96], visit, 0)
+        def single(s, carry, tiles=tiles, rel=rel, multiply=multiply):
+            tile_copy(tiles, rel * slots, s).wait()
+            multiply(s)
+            return carry
+
+        groups = lax.div(index[96], UNROLL)
+        lax.fori_loop(0, groups, several, 0)
+        lax.fori_loop(groups * UNROLL, index[96], single, 0)
     for chain, (send, keep) in enumerate(((send0, keep0), (send1, keep1))):
-        cols = slice(chain * 128, chain * 128 + 128)
+        part = pl.ds(ROWS[chain][0], ROWS[chain][1])
         for s, chip in enumerate(chip_slots(info, REDUCE[chain])):
             for rel in range(2):
                 block = chip * 2 + (core if rel == 0 else 1 - core)
                 if s < 4:
-                    keep[s, rel] = acc[block, :, cols]
+                    keep[s, rel] = acc[block, part, :]
                 else:
-                    send[s - 4, rel] = acc[block, :, cols].astype(jnp.bfloat16)
+                    send[s - 4, rel] = acc[block, part, :].astype(jnp.bfloat16)
 
 
 def spread(info, work, pieces):
     (index0, tiles0), (index1, tiles1) = work
     slots, edge, _ = tiles0.shape
-    quarter = (4, 2, edge, 128)
     return pl.pallas_call(
         spread_kernel,
         out_shape=[
-            jax.ShapeDtypeStruct(quarter, jnp.bfloat16),
-            jax.ShapeDtypeStruct(quarter, jnp.float32),
-        ]
-        * 2,
+            jax.ShapeDtypeStruct((4, 2, rows, 256), dtype)
+            for _, rows in ROWS
+            for dtype in (jnp.bfloat16, jnp.float32)
+        ],
         in_specs=[SMEM] * 3 + [ANY] * 6,
         out_specs=[VMEM] * 4,
         scratch_shapes=[
@@ -204,7 +225,7 @@
             pltpu.SemaphoreType.DMA((2 * slots,)),
             pltpu.SemaphoreType.DMA((2, 16)),
         ],
-        compiler_params=params(36),
+        compiler_params=params(60),
         cost_estimate=pl.CostEstimate(
             flops=2 * 47 * edge * edge * 512, bytes_accessed=20 * MIB, transcendentals=0
         ),
@@ -239,13 +260,13 @@
 
 def last_join_kernel(keep0, got0, keep1, got1, own, other):
     for chain, (keep, got) in enumerate(((keep0, got0), (keep1, got1))):
-        cols = slice(chain * 128, chain * 128 + 128)
-        own[:, cols] = keep[0, 0] + got[0, 0].astype(jnp.float32)
-        other[:, cols] = keep[0, 1] + got[0, 1].astype(jnp.float32)
+        part = pl.ds(ROWS[chain][0], ROWS[chain][1])
+        own[part, :] = keep[0, 0] + got[0, 0].astype(jnp.float32)
+        other[part, :] = keep[0, 1] + got[0, 1].astype(jnp.float32)
 
 
 def last_join(keep0, got0, keep1, got1):
-    edge = keep0.shape[2]
+    edge = keep0.shape[2] + keep1.shape[2]
     return pl.pallas_call(
         last_join_kernel,
         out_shape=[jax.ShapeDtypeStruct((edge, 256), jnp.float32)] * 2,
@@ -256,26 +277,31 @@
     )(keep0, got0, keep1, got1)
 
 
-def aggregate(info, work, own_half, other_half, stages, state):
-    arrived = swap(other_half)
+def aggregate(info, work, own_half, arrived, stages, state):
+    def beside(k, values, state):
+        if k not in stages:
+            return values, state
+        return lax.optimization_barrier((values, stages[k](state)))
+
     pair = jnp.stack([own_half, arrived])
     have = [pair[None, :, first : first + rows] for first, rows in ROWS]
     for k in range(4):
         got = [exchange(h, steps[k]) for h, steps in zip(have, GATHER)]
-        if stages[k] is not None:
-            state = stages[k](state)
-            got, state = lax.optimization_barrier((got, state))
+        got, state = beside(k, got, state)
         if k < 3:
             have = [jnp.concatenate([h, g]) for h, g in zip(have, got)]
             have = lax.optimization_barrier(have)
-    send0, keep0, send1, keep1 = spread(info, work, (have[0], got[0], have[1], got[1]))
-    send, keep = [send0, send1], [keep0, keep1]
+    parts = spread(info, work, (have[0], got[0], have[1], got[1]))
+    parts, state = beside(4, parts, state)
+    send, keep = [parts[0], parts[2]], [parts[1], parts[3]]
     for k in range(2):
         arrived = [exchange(send[chain], REDUCE[chain][k]) for chain in range(2)]
         arrived = lax.optimization_barrier(arrived)
+        arrived, state = beside(5 + k, arrived, state)
         for chain in range(2):
             send[chain], keep[chain] = join(keep[chain], arrived[chain])
     arrived = [exchange(send[chain], REDUCE[chain][2]) for chain in range(2)]
+    arrived, state = beside(7, arrived, state)
     own, other = last_join(keep[0], arrived[0], keep[1], arrived[1])
     return own, swap(other), state
 
@@ -388,25 +414,70 @@
         send, rest = weight_blocks(info, keep, got)
         return rest + exchange(send, steps[0]), own_term
 
-    def middle(state):
-        total, own_term = state
-        total = total[:2] + exchange(total[2:], steps[1])
-        return total[0] + exchange(total[1], steps[2]), own_term
-
-    def last(state):
-        total, own_term = state
-        for step in ROW_SUM:
-            total = total + exchange(total, step)
-        return total, own_term
-
-    return (local, first, middle, last)
-
-
-def split_weights(total):
-    every = lax.all_gather(total, "col", axis=0, tiled=False)
-    width = total.shape[1]
-    both = every.reshape(8, 2, 64, width)
-    return both[:, 0].reshape(-1, width), both[:, 1].reshape(-1, width)
+    def halve(step):
+        def stage(state):
+            total, own_term = state
+            half = total.shape[0] // 2
+            return total[:half] + exchange(total[half:], step), own_term
+
+        return stage
+
+    def row_sum(*chosen):
+        def stage(state):
+            total, own_term = state
+            for step in chosen:
+                total = total + exchange(total, step)
+            return total, own_term
+
+        return stage
+
+    def collect(*chosen):
+        def stage(state):
+            total, own_term = state
+            for step in chosen:
+                total = jnp.concatenate([total, exchange(total, step)])
+            return total, own_term
+
+        return stage
+
+    l_and_y = (halve(steps[2]), row_sum(ROW_SUM[0]))
+    return {
+        0: local,
+        1: first,
+        2: halve(steps[1]),
+        3: lambda state: l_and_y[1](l_and_y[0](state)),
+        4: row_sum(ROW_SUM[1]),
+        5: row_sum(*ROW_SUM[2:]),
+        6: collect(steps[2], steps[1]),
+        7: collect(steps[0]),
+    }
+
+
+def both_weights_kernel(info, mine, theirs, grad_self, grad_neigh):
+    core = info[4]
+    for value, owner in ((mine, core), (theirs, 1 - core)):
+        for s, chip in enumerate(chip_slots(info, REDUCE[0], owner)):
+            rows = pl.ds(pl.multiple_of(chip * 64, 64), 64)
+
+            @pl.when(owner == 0)
+            def _(value=value, s=s, rows=rows):
+                grad_self[rows, :] = value[s]
+
+            @pl.when(owner == 1)
+            def _(value=value, s=s, rows=rows):
+                grad_neigh[rows, :] = value[s]
+
+
+def both_weights(info, total):
+    width = total.shape[2]
+    return pl.pallas_call(
+        both_weights_kernel,
+        out_shape=[jax.ShapeDtypeStruct((8 * total.shape[1], width), jnp.float32)] * 2,
+        in_specs=[SMEM, VMEM, VMEM],
+        out_specs=[VMEM] * 2,
+        compiler_params=params(16),
+        name="both_weights",
+    )(info, total, swap(total))
 
 
 def finish_kernel(info, own_term, own, got, out):
@@ -429,11 +500,12 @@
     core = col % 2
     info = jnp.stack([row // 4, row % 4, col // 4, col // 2 % 2, core]).astype(jnp.int32)
     index = jnp.concatenate([tile_dst, tile_src, tile_count])
-    work = ((index, tile_values), (swap(index), swap(tile_values)))
-
     first = core == 0
     mine = jnp.where(first, features[:, :256], features[:, 256:])
     theirs = jnp.where(first, features[:, 256:], features[:, :256])
+    theirs = swap(theirs)
+    theirs, tiles = lax.optimization_barrier((theirs, tile_values))
+    work = ((index, tile_values), (swap(index), swap(tiles)))
     own, got, degree = aggregate(
         info, work, mine, theirs, degree_stages(info, index, tile_values), None
     )
@@ -442,9 +514,9 @@
         info, features, cotangent, w_self, w_neigh, degree, own, got
     )
     own, got, (total, own_term) = aggregate(
-        info, work, mine, theirs, weight_stages(info, features, w_self), (grad_pre, mean)
-    )
-    grad_self, grad_neigh = split_weights(total)
+        info, work, mine, swap(theirs), weight_stages(info, features, w_self), (grad_pre, mean)
+    )
+    grad_self, grad_neigh = both_weights(info, total)
     grad_features = finish(info, own_term, own, got)
     return (output, grad_features, grad_self, grad_neigh)
 

time: 296 us -> 241 us (0.81); the launches traced: 292 us -> 241 us
  waiting for transfers between devices: 138 us -> 107 us
  Pallas kernels: 37.3 us -> 23.6 us
  between operations: 15.2 us -> 1.92 us
  starting transfers between devices: 88 us -> 96 us
    ppermute x46 -> x50, waiting for transfers between devices: 138 us -> 107 us  [exchange(): return lax.ppermute(value, BOTH, pairs)]
    pallas_call x2 -> x3, Pallas kernels: 25.2 us -> 16.5 us  [the longest x2 14.4 us: spread(): pl.pallas_call(spread_kernel, out_shape=[jax.ShapeDtypeStruct((4, 2, rows...]
    ppermute x46 -> x50, starting transfers between devices: 88 us -> 96 us  [exchange(): return lax.ppermute(value, BOTH, pairs)]
    pallas_call x1, Pallas kernels: 6.38 us -> 1.39 us  [partial_degree(): pl.pallas_call(degree_kernel, out_shape=[jax.ShapeDtypeStruct((8, 8, edge...]
    slice x2, local copies, waits for them, and re-layouts: 3.11 us -> 0.03 us  [stage(): return (total[:half] + exchange(total[half:], step), own_term)]
    unnamed x24 -> x48, local copies, waits for them, and re-layouts: 5.63 us -> 8.17 us
  transfers between devices with their start and end apart: 47 -> 50, of which waited for: 31 -> 27; matrix products, arithmetic and copies ran while one was open for 1% -> 1% of each run, Pallas kernels for 7% -> 4%
where the time goes in v2:
time: 241 us
  waiting for transfers between devices  107 us (44%)
  starting transfers between devices  96 us (40%)
  Pallas kernels  23.6 us (10%)
  local copies, waits for them, and re-layouts  8.38 us (3%)
  other arithmetic  3.81 us (2%)
    ppermute x50, waiting for transfers between devices, exchange(): return lax.ppermute(value, BOTH, pairs)  107 us
    ppermute x50, starting transfers between devices, exchange(): return lax.ppermute(value, BOTH, pairs)  96 us
    pallas_call x2, Pallas kernels, spread(): pl.pallas_call(spread_kernel, out_shape=[jax.ShapeDtypeStruct((4, 2, rows...  14.4 us
    unnamed x48, local copies, waits for them, and re-layouts  8.17 us
  transfers between devices with their start and end apart: 50, of which 27 were waited for; matrix products, arithmetic and copies ran while one was open for 1% of the time, Pallas kernels for 4%

profile of v2, /device:TPU:1, one launch (start us, length us, event | category | flops | bytes accessed | tf_op | source)
XLA Modules:
  0.0 240.5 jit_solution(4718143206010954191)
XLA Ops:
  1.7 3.3 %collective-permute-start = (bf16[256,256]{1,0:T(8,128)(2,1)S(1)}, bf16[256,256]{1,0:T(8,128)(2,1)S(1)}, u32[]{:S(2)}, u32[]{:S(2)}) collective-permute-start(bf16[256,256]{1,0:T(8,128)(2,1)S(1)} %get-tuple-element.220), channel_id=1, source_target_pairs={{0,1},{1,0},{2,3},{3,2},{4,5},{5,4},{6,7},{7,6},{8,9},{9,8},{10,11... | collective-permute-start | bytes 393224 | tf_op jit(solution)/shard_map/ppermute | solution.py:42
  7.4 6.1 %collective-permute-start.1 = (bf16[1,2,176,256]{3,2,1,0:T(8,128)(2,1)S(1)}, bf16[1,2,176,256]{3,2,1,0:T(8,128)(2,1)S(1)}, u32[]{:S(2)}, u32[]{:S(2)}) collective-permute-start(bf16[1,2,176,256]{3,2,1,0:T(8,128)(2,1)S(1)} %fusion.3), channel_id=1, source_target_pairs={{0,16},{1,49},{2,18},{3,51},{4,20},{5,53},{6,22},{7,55},{8,24},{9,... | collective-permute-start | bytes 540680 | tf_op jit(solution)/shard_map/ppermute | solution.py:42
  13.5 4.3 %collective-permute-done.1 = bf16[1,2,176,256]{3,2,1,0:T(8,128)(2,1)S(1)} collective-permute-done((bf16[1,2,176,256]{3,2,1,0:T(8,128)(2,1)S(1)}, bf16[1,2,176,256]{3,2,1,0:T(8,128)(2,1)S(1)}, u32[]{:S(2)}, u32[]{:S(2)}) %collective-permute-start.1) | collective-permute-done | bytes 180256 | tf_op jit(solution)/shard_map/ppermute | solution.py:42
  24.7 3.9 %collective-permute-start.5 = (f32[8,8,256]{2,1,0:T(8,128)S(1)}, f32[8,8,256]{2,1,0:T(8,128)S(1)}, u32[]{:S(2)}, u32[]{:S(2)}) collective-permute-start(f32[8,8,256]{2,1,0:T(8,128)S(1)} %get-tuple-element.116), channel_id=1, source_target_pairs={{0,1},{1,0},{2,3},{3,2},{4,5},{5,4},{6,7},{7,6},{8,9},{9,8},{10,11... | collective-permute-start | bytes 196616 | tf_op jit(solution)/shard_map/ppermute | solution.py:42
  32.4 3.2 %collective-permute-start.7 = (bf16[4,2,80,256]{3,2,1,0:T(8,128)(2,1)S(1)}, bf16[4,2,80,256]{3,2,1,0:T(8,128)(2,1)S(1)}, u32[]{:S(2)}, u32[]{:S(2)}) collective-permute-start(bf16[4,2,80,256]{3,2,1,0:T(8,128)(2,1)S(1)} %pad_maximum_fusion.10), channel_id=1, source_target_pairs={{0,16},{1,49},{2,18},{3,51},{4,20},{5,53},{6,22},{7,55},{8,24},{9,... | collective-permute-start | bytes 983048 | tf_op jit(solution)/shard_map/ppermute | solution.py:42
  35.7 2.9 %collective-permute-done.9 = f32[2,8,256]{2,1,0:T(8,128)S(1)} collective-permute-done((f32[2,8,256]{2,1,0:T(8,128)S(1)}, f32[2,8,256]{2,1,0:T(8,128)S(1)}, u32[]{:S(2)}, u32[]{:S(2)}) %collective-permute-start.9) | collective-permute-done | bytes 16416 | tf_op jit(solution)/shard_map/ppermute | solution.py:42
  38.6 3.3 %collective-permute-done.7 = bf16[4,2,80,256]{3,2,1,0:T(8,128)(2,1)S(1)} collective-permute-done((bf16[4,2,80,256]{3,2,1,0:T(8,128)(2,1)S(1)}, bf16[4,2,80,256]{3,2,1,0:T(8,128)(2,1)S(1)}, u32[]{:S(2)}, u32[]{:S(2)}) %collective-permute-start.7) | collective-permute-done | bytes 327712 | tf_op jit(solution)/shard_map/ppermute | solution.py:42
  46.0 5.4 %collective-permute-start.13 = (s32[97]{0:T(128)S(1)}, s32[97]{0:T(128)S(1)}, u32[]{:S(2)}, u32[]{:S(2)}) collective-permute-start(s32[97]{0:T(128)S(1)} %pad_add_fusion.index.index0), channel_id=1, source_target_pairs={{0,1},{1,0},{2,3},{3,2},{4,5},{5,4},{6,7},{7,6},{8,9},{9,8},{10,11... | collective-permute-start | bytes 1172 | tf_op jit(solution)/shard_map/ppermute | solution.py:42
  51.4 3.5 %collective-permute-done.12 = f32[1,8,256]{2,1,0:T(8,128)S(1)} collective-permute-done((f32[1,8,256]{2,1,0:T(8,128)S(1)}, f32[1,8,256]{2,1,0:T(8,128)S(1)}, u32[]{:S(2)}, u32[]{:S(2)}) %collective-permute-start.12) | collective-permute-done | bytes 8224 | tf_op jit(solution)/shard_map/ppermute | solution.py:42
  54.9 6.6 %collective-permute-done.11.refs_3_ = bf16[8,2,80,256]{3,2,1,0:T(8,128)(2,1)S(1)} collective-permute-done((bf16[8,2,80,256]{3,2,1,0:T(8,128)(2,1)S(1)}, bf16[8,2,80,256]{3,2,1,0:T(8,128)(2,1)S(1)}, u32[]{:S(2)}, u32[]{:S(2)}) %collective-permute-start.11) | collective-permute-done | bytes 655392 | tf_op jit(solution)/shard_map/ppermute | solution.py:42
  62.9 7.2 %spread.2 = (bf16[4,2,176,256]{3,2,1,0:T(8,128)(2,1)}, f32[4,2,176,256]{3,2,1,0:T(8,128)}, bf16[4,2,80,256]{3,2,1,0:T(8,128)(2,1)}, f32[4,2,80,256]{3,2,1,0:T(8,128)}) custom-call(s32[5]{0:T(128)} %copy-done.9, s32[97]{0:T(128)} %copy-done.12, s32[97]{0:T(128)} %copy-done.21, bf16[48,256,256]{2,1,0:T(8,128)(2,1)} %tiles0.3, ...), custom_call_target="tpu_custom_call" | custom-call | flops 3154116608 | bytes 20971520 | tf_op jit(solution)/shard_map/spread/pallas_call | solution.py:212
  73.9 5.3 %collective-permute-done.16.got = bf16[4,2,80,256]{3,2,1,0:T(8,128)(2,1)S(1)} collective-permute-done((bf16[4,2,80,256]{3,2,1,0:T(8,128)(2,1)}, bf16[4,2,80,256]{3,2,1,0:T(8,128)(2,1)S(1)}, u32[]{:S(2)}, u32[]{:S(2)}) %collective-permute-start.16) | collective-permute-done | bytes 327712 | tf_op jit(solution)/shard_map/ppermute | solution.py:42
  86.3 3.5 %collective-permute-done.18.got = bf16[2,2,80,256]{3,2,1,0:T(8,128)(2,1)S(1)} collective-permute-done((bf16[2,2,80,256]{3,2,1,0:T(8,128)(2,1)S(1)}, bf16[2,2,80,256]{3,2,1,0:T(8,128)(2,1)S(1)}, u32[]{:S(2)}, u32[]{:S(2)}) %collective-permute-start.18) | collective-permute-done | bytes 163872 | tf_op jit(solution)/shard_map/ppermute | solution.py:42
  89.9 3.5 %collective-permute-start.19 = (bf16[1,2,176,256]{3,2,1,0:T(8,128)(2,1)S(1)}, bf16[1,2,176,256]{3,2,1,0:T(8,128)(2,1)S(1)}, u32[]{:S(2)}, u32[]{:S(2)}) collective-permute-start(bf16[1,2,176,256]{3,2,1,0:T(8,128)(2,1)S(1)} %get-tuple-element.142), channel_id=1, source_target_pairs={{0,2},{1,3},{2,0},{3,1},{4,6},{5,7},{6,4},{7,5},{8,10},{9,11},{10,... | collective-permute-start | bytes 540680 | tf_op jit(solution)/shard_map/ppermute | solution.py:42
  93.5 3.5 %collective-permute-done.20.got1 = bf16[1,2,80,256]{3,2,1,0:T(8,128)(2,1)S(1)} collective-permute-done((bf16[1,2,80,256]{3,2,1,0:T(8,128)(2,1)S(1)}, bf16[1,2,80,256]{3,2,1,0:T(8,128)(2,1)S(1)}, u32[]{:S(2)}, u32[]{:S(2)}) %collective-permute-start.20) | collective-permute-done | bytes 81952 | tf_op jit(solution)/shard_map/ppermute | solution.py:42
  97.1 8.5 %collective-permute-start.21 = (f32[256,256]{1,0:T(8,128)S(1)}, f32[256,256]{1,0:T(8,128)S(1)}, u32[]{:S(2)}, u32[]{:S(2)}) collective-permute-start(f32[256,256]{1,0:T(8,128)S(1)} %get-tuple-element.148), channel_id=1, source_target_pairs={{0,1},{1,0},{2,3},{3,2},{4,5},{5,4},{6,7},{7,6},{8,9},{9,8},{10,11... | collective-permute-start | bytes 786440 | tf_op jit(solution)/shard_map/ppermute | solution.py:42
  113.0 3.5 %collective-permute-start.23 = (bf16[1,2,176,256]{3,2,1,0:T(8,128)(2,1)S(1)}, bf16[1,2,176,256]{3,2,1,0:T(8,128)(2,1)S(1)}, u32[]{:S(2)}, u32[]{:S(2)}) collective-permute-start(bf16[1,2,176,256]{3,2,1,0:T(8,128)(2,1)S(1)} %fusion.1), channel_id=1, source_target_pairs={{0,16},{1,49},{2,18},{3,51},{4,20},{5,53},{6,22},{7,55},{8,24},{9,... | collective-permute-start | bytes 540680 | tf_op jit(solution)/shard_map/ppermute | solution.py:42
  117.1 3.9 %collective-permute-done.24 = bf16[1,2,80,256]{3,2,1,0:T(8,128)(2,1)S(1)} collective-permute-done((bf16[1,2,80,256]{3,2,1,0:T(8,128)(2,1)S(1)}, bf16[1,2,80,256]{3,2,1,0:T(8,128)(2,1)S(1)}, u32[]{:S(2)}, u32[]{:S(2)}) %collective-permute-start.24) | collective-permute-done | bytes 81952 | tf_op jit(solution)/shard_map/ppermute | solution.py:42
  124.5 6.9 %collective-permute-done.28 = f32[4,64,512]{2,1,0:T(8,128)S(1)} collective-permute-done((f32[4,64,512]{2,1,0:T(8,128)S(1)}, f32[4,64,512]{2,1,0:T(8,128)S(1)}, u32[]{:S(2)}, u32[]{:S(2)}) %collective-permute-start.28) | collective-permute-done | bytes 524320 | tf_op jit(solution)/shard_map/ppermute | solution.py:42
  131.4 4.0 %collective-permute-done.26 = bf16[2,2,176,256]{3,2,1,0:T(8,128)(2,1)S(1)} collective-permute-done((bf16[2,2,176,256]{3,2,1,0:T(8,128)(2,1)S(1)}, bf16[2,2,176,256]{3,2,1,0:T(8,128)(2,1)S(1)}, u32[]{:S(2)}, u32[]{:S(2)}) %collective-permute-start.26) | collective-permute-done | bytes 360480 | tf_op jit(solution)/shard_map/ppermute | solution.py:42
  135.8 3.8 %collective-permute-start.30 = (bf16[4,2,80,256]{3,2,1,0:T(8,128)(2,1)S(1)}, bf16[4,2,80,256]{3,2,1,0:T(8,128)(2,1)S(1)}, u32[]{:S(2)}, u32[]{:S(2)}) collective-permute-start(bf16[4,2,80,256]{3,2,1,0:T(8,128)(2,1)S(1)} %pad_maximum_fusion.11), channel_id=1, source_target_pairs={{0,16},{1,49},{2,18},{3,51},{4,20},{5,53},{6,22},{7,55},{8,24},{9,... | collective-permute-start | bytes 983048 | tf_op jit(solution)/shard_map/ppermute | solution.py:42
  141.3 4.5 %collective-permute-done.30 = bf16[4,2,80,256]{3,2,1,0:T(8,128)(2,1)S(1)} collective-permute-done((bf16[4,2,80,256]{3,2,1,0:T(8,128)(2,1)S(1)}, bf16[4,2,80,256]{3,2,1,0:T(8,128)(2,1)S(1)}, u32[]{:S(2)}, u32[]{:S(2)}) %collective-permute-start.30) | collective-permute-done | bytes 327712 | tf_op jit(solution)/shard_map/ppermute | solution.py:42
  149.5 13.0 %collective-permute-done.34 = f32[1,64,512]{2,1,0:T(8,128)S(1)} collective-permute-done((f32[1,64,512]{2,1,0:T(8,128)S(1)}, f32[1,64,512]{2,1,0:T(8,128)S(1)}, u32[]{:S(2)}, u32[]{:S(2)}) %collective-permute-start.34) | collective-permute-done | bytes 131104 | tf_op jit(solution)/shard_map/ppermute | solution.py:42
  162.4 5.2 %collective-permute-start.35 = (f32[1,64,512]{2,1,0:T(8,128)S(1)}, f32[1,64,512]{2,1,0:T(8,128)S(1)}, u32[]{:S(2)}, u32[]{:S(2)}) collective-permute-start(f32[1,64,512]{2,1,0:T(8,128)S(1)} %slice_add_fusion.1), channel_id=1, source_target_pairs={{0,64},{1,193},{2,66},{3,195},{4,68},{5,197},{6,70},{7,199},{8,72}... | collective-permute-start | bytes 393224 | tf_op jit(solution)/shard_map/ppermute | solution.py:42
  172.8 7.2 %spread.3 = (bf16[4,2,176,256]{3,2,1,0:T(8,128)(2,1)}, f32[4,2,176,256]{3,2,1,0:T(8,128)}, bf16[4,2,80,256]{3,2,1,0:T(8,128)(2,1)}, f32[4,2,80,256]{3,2,1,0:T(8,128)}) custom-call(s32[5]{0:T(128)} %copy-done.9, s32[97]{0:T(128)} %copy-done.12, s32[97]{0:T(128)} %copy-done.21, bf16[48,256,256]{2,1,0:T(8,128)(2,1)} %tiles0.3, ...), custom_call_target="tpu_custom_call" | custom-call | flops 3154116608 | bytes 20971520 | tf_op jit(solution)/shard_map/spread/pallas_call | solution.py:212
  181.0 2.9 %collective-permute-start.37 = (bf16[4,2,176,256]{3,2,1,0:T(8,128)(2,1)}, bf16[4,2,176,256]{3,2,1,0:T(8,128)(2,1)S(1)}, u32[]{:S(2)}, u32[]{:S(2)}) collective-permute-start(bf16[4,2,176,256]{3,2,1,0:T(8,128)(2,1)} %get-tuple-element.187), channel_id=1, source_target_pairs={{0,4},{1,13},{2,6},{3,15},{4,0},{5,9},{6,2},{7,11},{8,12},{9,5},{1... | collective-permute-start | bytes 2162696 | tf_op jit(solution)/shard_map/ppermute | solution.py:42
  187.4 6.1 %collective-permute-done.39 = f32[1,64,512]{2,1,0:T(8,128)S(1)} collective-permute-done((f32[1,64,512]{2,1,0:T(8,128)S(1)}, f32[1,64,512]{2,1,0:T(8,128)S(1)}, u32[]{:S(2)}, u32[]{:S(2)}) %collective-permute-start.39) | collective-permute-done | bytes 131104 | tf_op jit(solution)/shard_map/ppermute | solution.py:42
  193.6 6.9 %collective-permute-done.40 = f32[1,64,512]{2,1,0:T(8,128)S(1)} collective-permute-done((f32[1,64,512]{2,1,0:T(8,128)S(1)}, f32[1,64,512]{2,1,0:T(8,128)S(1)}, u32[]{:S(2)}, u32[]{:S(2)}) %collective-permute-start.40) | collective-permute-done | bytes 131104 | tf_op jit(solution)/shard_map/ppermute | solution.py:42
  206.4 3.2 %collective-permute-start.42 = (bf16[2,2,80,256]{3,2,1,0:T(8,128)(2,1)S(1)}, bf16[2,2,80,256]{3,2,1,0:T(8,128)(2,1)S(1)}, u32[]{:S(2)}, u32[]{:S(2)}) collective-permute-start(bf16[2,2,80,256]{3,2,1,0:T(8,128)(2,1)S(1)} %get-tuple-element.198), channel_id=1, source_target_pairs={{0,4},{1,13},{2,6},{3,15},{4,0},{5,9},{6,2},{7,11},{8,12},{9,5},{1... | collective-permute-start | bytes 491528 | tf_op jit(solution)/shard_map/ppermute | solution.py:42
  212.4 4.0 %collective-permute-start.47 = (f32[4,64,512]{2,1,0:T(8,128)S(1)}, f32[4,64,512]{2,1,0:T(8,128)S(1)}, u32[]{:S(2)}, u32[]{:S(2)}) collective-permute-start(f32[4,64,512]{2,1,0:T(8,128)S(1)} %pad_maximum_fusion.7), channel_id=1, source_target_pairs={{0,4},{1,13},{2,6},{3,15},{4,0},{5,9},{6,2},{7,11},{8,12},{9,5},{1... | collective-permute-start | bytes 1572872 | tf_op jit(solution)/shard_map/ppermute | solution.py:42
  217.5 8.9 %collective-permute-done.47 = f32[4,64,512]{2,1,0:T(8,128)S(1)} collective-permute-done((f32[4,64,512]{2,1,0:T(8,128)S(1)}, f32[4,64,512]{2,1,0:T(8,128)S(1)}, u32[]{:S(2)}, u32[]{:S(2)}) %collective-permute-start.47) | collective-permute-done | bytes 524320 | tf_op jit(solution)/shard_map/ppermute | solution.py:42
  226.5 7.9 %collective-permute-start.49 = (f32[8,64,512]{2,1,0:T(8,128)S(1)}, f32[8,64,512]{2,1,0:T(8,128)S(1)}, u32[]{:S(2)}, u32[]{:S(2)}) collective-permute-start(f32[8,64,512]{2,1,0:T(8,128)S(1)} %pad_maximum_fusion.2.mine), channel_id=1, source_target_pairs={{0,1},{1,0},{2,3},{3,2},{4,5},{5,4},{6,7},{7,6},{8,9},{9,8},{10,11... | collective-permute-start | bytes 3145736 | tf_op jit(solution)/shard_map/ppermute | solution.py:42
  (174 shorter events, 72.8 us)
Async XLA Ops:
  6.0 56.4 %collective-permute-start.14 = (bf16[48,256,256]{2,1,0:T(8,128)(2,1)}, bf16[48,256,256]{2,1,0:T(8,128)(2,1)}, u32[]{:S(2)}, u32[]{:S(2)}) collective-permute-start(bf16[48,256,256]{2,1,0:T(8,128)(2,1)} %tiles0.3), channel_id=1, source_target_pairs={{0,1},{1,0},{2,3},{3,2},{4,5},{5,4},{6,7},{7,6},{8,9},{9,8},{10,11... | collective-permute-start | bytes 18874376 | tf_op jit(solution)/shard_map/ppermute | solution.py:42
  7.4 10.5 %collective-permute-start.1 = (bf16[1,2,176,256]{3,2,1,0:T(8,128)(2,1)S(1)}, bf16[1,2,176,256]{3,2,1,0:T(8,128)(2,1)S(1)}, u32[]{:S(2)}, u32[]{:S(2)}) collective-permute-start(bf16[1,2,176,256]{3,2,1,0:T(8,128)(2,1)S(1)} %fusion.3), channel_id=1, source_target_pairs={{0,16},{1,49},{2,18},{3,51},{4,20},{5,53},{6,22},{7,55},{8,24},{9,... | collective-permute-start | bytes 540680 | tf_op jit(solution)/shard_map/ppermute | solution.py:42
  17.9 11.6 %collective-permute-start.3 = (bf16[2,2,176,256]{3,2,1,0:T(8,128)(2,1)S(1)}, bf16[2,2,176,256]{3,2,1,0:T(8,128)(2,1)S(1)}, u32[]{:S(2)}, u32[]{:S(2)}) collective-permute-start(bf16[2,2,176,256]{3,2,1,0:T(8,128)(2,1)S(1)} %pad_maximum_fusion.8), channel_id=1, source_target_pairs={{0,48},{1,17},{2,50},{3,19},{4,52},{5,21},{6,54},{7,23},{8,56},{9,... | collective-permute-start | bytes 1081352 | tf_op jit(solution)/shard_map/ppermute | solution.py:42
  20.3 9.1 %collective-permute-start.4 = (bf16[2,2,80,256]{3,2,1,0:T(8,128)(2,1)S(1)}, bf16[2,2,80,256]{3,2,1,0:T(8,128)(2,1)S(1)}, u32[]{:S(2)}, u32[]{:S(2)}) collective-permute-start(bf16[2,2,80,256]{3,2,1,0:T(8,128)(2,1)S(1)} %pad_maximum_fusion.13), channel_id=1, source_target_pairs={{0,192},{1,65},{2,194},{3,67},{4,196},{5,69},{6,198},{7,71},{8,200... | collective-permute-start | bytes 491528 | tf_op jit(solution)/shard_map/ppermute | solution.py:42
  29.6 12.3 %collective-permute-start.6 = (bf16[4,2,176,256]{3,2,1,0:T(8,128)(2,1)S(1)}, bf16[4,2,176,256]{3,2,1,0:T(8,128)(2,1)S(1)}, u32[]{:S(2)}, u32[]{:S(2)}) collective-permute-start(bf16[4,2,176,256]{3,2,1,0:T(8,128)(2,1)S(1)} %pad_maximum_fusion.3), channel_id=1, source_target_pairs={{0,64},{1,193},{2,66},{3,195},{4,68},{5,197},{6,70},{7,199},{8,72}... | collective-permute-start | bytes 2162696 | tf_op jit(solution)/shard_map/ppermute | solution.py:42
  32.4 9.5 %collective-permute-start.7 = (bf16[4,2,80,256]{3,2,1,0:T(8,128)(2,1)S(1)}, bf16[4,2,80,256]{3,2,1,0:T(8,128)(2,1)S(1)}, u32[]{:S(2)}, u32[]{:S(2)}) collective-permute-start(bf16[4,2,80,256]{3,2,1,0:T(8,128)(2,1)S(1)} %pad_maximum_fusion.10), channel_id=1, source_target_pairs={{0,16},{1,49},{2,18},{3,51},{4,20},{5,53},{6,22},{7,55},{8,24},{9,... | collective-permute-start | bytes 983048 | tf_op jit(solution)/shard_map/ppermute | solution.py:42
  42.1 19.4 %collective-permute-start.10 = (bf16[8,2,176,256]{3,2,1,0:T(8,128)(2,1)S(1)}, bf16[8,2,176,256]{3,2,1,0:T(8,128)(2,1)S(1)}, u32[]{:S(2)}, u32[]{:S(2)}) collective-permute-start(bf16[8,2,176,256]{3,2,1,0:T(8,128)(2,1)S(1)} %pad_maximum_fusion.refs_0_), channel_id=1, source_target_pairs={{0,192},{1,65},{2,194},{3,67},{4,196},{5,69},{6,198},{7,71},{8,200... | collective-permute-start | bytes 4325384 | tf_op jit(solution)/shard_map/ppermute | solution.py:42
  43.8 17.7 %collective-permute-start.11 = (bf16[8,2,80,256]{3,2,1,0:T(8,128)(2,1)S(1)}, bf16[8,2,80,256]{3,2,1,0:T(8,128)(2,1)S(1)}, u32[]{:S(2)}, u32[]{:S(2)}) collective-permute-start(bf16[8,2,80,256]{3,2,1,0:T(8,128)(2,1)S(1)} %pad_maximum_fusion.5.refs_2_), channel_id=1, source_target_pairs={{0,48},{1,17},{2,50},{3,19},{4,52},{5,21},{6,54},{7,23},{8,56},{9,... | collective-permute-start | bytes 1966088 | tf_op jit(solution)/shard_map/ppermute | solution.py:42
  45.6 9.3 %collective-permute-start.12 = (f32[1,8,256]{2,1,0:T(8,128)S(1)}, f32[1,8,256]{2,1,0:T(8,128)S(1)}, u32[]{:S(2)}, u32[]{:S(2)}) collective-permute-start(f32[1,8,256]{2,1,0:T(8,128)S(1)} %slice.62), channel_id=1, source_target_pairs={{0,2},{1,3},{2,0},{3,1},{4,6},{5,7},{6,4},{7,5},{8,10},{9,11},{10,... | collective-permute-start | bytes 24584 | tf_op jit(solution)/shard_map/ppermute | solution.py:42
  46.0 15.5 %collective-permute-start.13 = (s32[97]{0:T(128)S(1)}, s32[97]{0:T(128)S(1)}, u32[]{:S(2)}, u32[]{:S(2)}) collective-permute-start(s32[97]{0:T(128)S(1)} %pad_add_fusion.index.index0), channel_id=1, source_target_pairs={{0,1},{1,0},{2,3},{3,2},{4,5},{5,4},{6,7},{7,6},{8,9},{9,8},{10,11... | collective-permute-start | bytes 1172 | tf_op jit(solution)/shard_map/ppermute | solution.py:42
  70.1 11.6 %collective-permute-start.15 = (bf16[4,2,176,256]{3,2,1,0:T(8,128)(2,1)}, bf16[4,2,176,256]{3,2,1,0:T(8,128)(2,1)S(1)}, u32[]{:S(2)}, u32[]{:S(2)}) collective-permute-start(bf16[4,2,176,256]{3,2,1,0:T(8,128)(2,1)} %get-tuple-element.132), channel_id=1, source_target_pairs={{0,4},{1,13},{2,6},{3,15},{4,0},{5,9},{6,2},{7,11},{8,12},{9,5},{1... | collective-permute-start | bytes 2162696 | tf_op jit(solution)/shard_map/ppermute | solution.py:42
  72.1 7.2 %collective-permute-start.16 = (bf16[4,2,80,256]{3,2,1,0:T(8,128)(2,1)}, bf16[4,2,80,256]{3,2,1,0:T(8,128)(2,1)S(1)}, u32[]{:S(2)}, u32[]{:S(2)}) collective-permute-start(bf16[4,2,80,256]{3,2,1,0:T(8,128)(2,1)} %get-tuple-element.133), channel_id=1, source_target_pairs={{0,2},{1,3},{2,0},{3,1},{4,6},{5,7},{6,4},{7,5},{8,10},{9,11},{10,... | collective-permute-start | bytes 983048 | tf_op jit(solution)/shard_map/ppermute | solution.py:42
  89.9 7.2 %collective-permute-start.19 = (bf16[1,2,176,256]{3,2,1,0:T(8,128)(2,1)S(1)}, bf16[1,2,176,256]{3,2,1,0:T(8,128)(2,1)S(1)}, u32[]{:S(2)}, u32[]{:S(2)}) collective-permute-start(bf16[1,2,176,256]{3,2,1,0:T(8,128)(2,1)S(1)} %get-tuple-element.142), channel_id=1, source_target_pairs={{0,2},{1,3},{2,0},{3,1},{4,6},{5,7},{6,4},{7,5},{8,10},{9,11},{10,... | collective-permute-start | bytes 540680 | tf_op jit(solution)/shard_map/ppermute | solution.py:42
  97.1 9.7 %collective-permute-start.21 = (f32[256,256]{1,0:T(8,128)S(1)}, f32[256,256]{1,0:T(8,128)S(1)}, u32[]{:S(2)}, u32[]{:S(2)}) collective-permute-start(f32[256,256]{1,0:T(8,128)S(1)} %get-tuple-element.148), channel_id=1, source_target_pairs={{0,1},{1,0},{2,3},{3,2},{4,5},{5,4},{6,7},{7,6},{8,9},{9,8},{10,11... | collective-permute-start | bytes 786440 | tf_op jit(solution)/shard_map/ppermute | solution.py:42
  110.0 11.0 %collective-permute-start.25 = (f32[512,512]{1,0:T(8,128)S(1)}, f32[512,512]{1,0:T(8,128)S(1)}, u32[]{:S(2)}, u32[]{:S(2)}) collective-permute-start(f32[512,512]{1,0:T(8,128)S(1)} %get-tuple-element.155), channel_id=1, source_target_pairs={{0,1},{1,0},{2,3},{3,2},{4,5},{5,4},{6,7},{7,6},{8,9},{9,8},{10,11... | collective-permute-start | bytes 3145736 | tf_op jit(solution)/shard_map/ppermute | solution.py:42
  113.0 8.0 %collective-permute-start.23 = (bf16[1,2,176,256]{3,2,1,0:T(8,128)(2,1)S(1)}, bf16[1,2,176,256]{3,2,1,0:T(8,128)(2,1)S(1)}, u32[]{:S(2)}, u32[]{:S(2)}) collective-permute-start(bf16[1,2,176,256]{3,2,1,0:T(8,128)(2,1)S(1)} %fusion.1), channel_id=1, source_target_pairs={{0,16},{1,49},{2,18},{3,51},{4,20},{5,53},{6,22},{7,55},{8,24},{9,... | collective-permute-start | bytes 540680 | tf_op jit(solution)/shard_map/ppermute | solution.py:42
  121.7 9.6 %collective-permute-start.28 = (f32[4,64,512]{2,1,0:T(8,128)S(1)}, f32[4,64,512]{2,1,0:T(8,128)S(1)}, u32[]{:S(2)}, u32[]{:S(2)}) collective-permute-start(f32[4,64,512]{2,1,0:T(8,128)S(1)} %get-tuple-element.164), channel_id=1, source_target_pairs={{0,4},{1,13},{2,6},{3,15},{4,0},{5,9},{6,2},{7,11},{8,12},{9,5},{1... | collective-permute-start | bytes 1572872 | tf_op jit(solution)/shard_map/ppermute | solution.py:42
  124.3 11.2 %collective-permute-start.26 = (bf16[2,2,176,256]{3,2,1,0:T(8,128)(2,1)S(1)}, bf16[2,2,176,256]{3,2,1,0:T(8,128)(2,1)S(1)}, u32[]{:S(2)}, u32[]{:S(2)}) collective-permute-start(bf16[2,2,176,256]{3,2,1,0:T(8,128)(2,1)S(1)} %pad_maximum_fusion.9), channel_id=1, source_target_pairs={{0,48},{1,17},{2,50},{3,19},{4,52},{5,21},{6,54},{7,23},{8,56},{9,... | collective-permute-start | bytes 1081352 | tf_op jit(solution)/shard_map/ppermute | solution.py:42
  135.5 11.4 %collective-permute-start.29 = (bf16[4,2,176,256]{3,2,1,0:T(8,128)(2,1)S(1)}, bf16[4,2,176,256]{3,2,1,0:T(8,128)(2,1)S(1)}, u32[]{:S(2)}, u32[]{:S(2)}) collective-permute-start(bf16[4,2,176,256]{3,2,1,0:T(8,128)(2,1)S(1)} %pad_maximum_fusion.4), channel_id=1, source_target_pairs={{0,64},{1,193},{2,66},{3,195},{4,68},{5,197},{6,70},{7,199},{8,72}... | collective-permute-start | bytes 2162696 | tf_op jit(solution)/shard_map/ppermute | solution.py:42
  135.8 10.0 %collective-permute-start.30 = (bf16[4,2,80,256]{3,2,1,0:T(8,128)(2,1)S(1)}, bf16[4,2,80,256]{3,2,1,0:T(8,128)(2,1)S(1)}, u32[]{:S(2)}, u32[]{:S(2)}) collective-permute-start(bf16[4,2,80,256]{3,2,1,0:T(8,128)(2,1)S(1)} %pad_maximum_fusion.11), channel_id=1, source_target_pairs={{0,16},{1,49},{2,18},{3,51},{4,20},{5,53},{6,22},{7,55},{8,24},{9,... | collective-permute-start | bytes 983048 | tf_op jit(solution)/shard_map/ppermute | solution.py:42
  147.2 23.5 %collective-permute-start.32 = (bf16[8,2,176,256]{3,2,1,0:T(8,128)(2,1)S(1)}, bf16[8,2,176,256]{3,2,1,0:T(8,128)(2,1)S(1)}, u32[]{:S(2)}, u32[]{:S(2)}) collective-permute-start(bf16[8,2,176,256]{3,2,1,0:T(8,128)(2,1)S(1)} %pad_maximum_fusion.1.refs_0_), channel_id=1, source_target_pairs={{0,192},{1,65},{2,194},{3,67},{4,196},{5,69},{6,198},{7,71},{8,200... | collective-permute-start | bytes 4325384 | tf_op jit(solution)/shard_map/ppermute | solution.py:42
  147.3 23.4 %collective-permute-start.33 = (bf16[8,2,80,256]{3,2,1,0:T(8,128)(2,1)S(1)}, bf16[8,2,80,256]{3,2,1,0:T(8,128)(2,1)S(1)}, u32[]{:S(2)}, u32[]{:S(2)}) collective-permute-start(bf16[8,2,80,256]{3,2,1,0:T(8,128)(2,1)S(1)} %pad_maximum_fusion.6.refs_2_), channel_id=1, source_target_pairs={{0,48},{1,17},{2,50},{3,19},{4,52},{5,21},{6,54},{7,23},{8,56},{9,... | collective-permute-start | bytes 1966088 | tf_op jit(solution)/shard_map/ppermute | solution.py:42
  148.1 14.3 %collective-permute-start.34 = (f32[1,64,512]{2,1,0:T(8,128)S(1)}, f32[1,64,512]{2,1,0:T(8,128)S(1)}, u32[]{:S(2)}, u32[]{:S(2)}) collective-permute-start(f32[1,64,512]{2,1,0:T(8,128)S(1)} %slice.69), channel_id=1, source_target_pairs={{0,2},{1,3},{2,0},{3,1},{4,6},{5,7},{6,4},{7,5},{8,10},{9,11},{10,... | collective-permute-start | bytes 393224 | tf_op jit(solution)/shard_map/ppermute | solution.py:42
  162.4 7.6 %collective-permute-start.35 = (f32[1,64,512]{2,1,0:T(8,128)S(1)}, f32[1,64,512]{2,1,0:T(8,128)S(1)}, u32[]{:S(2)}, u32[]{:S(2)}) collective-permute-start(f32[1,64,512]{2,1,0:T(8,128)S(1)} %slice_add_fusion.1), channel_id=1, source_target_pairs={{0,64},{1,193},{2,66},{3,195},{4,68},{5,197},{6,70},{7,199},{8,72}... | collective-permute-start | bytes 393224 | tf_op jit(solution)/shard_map/ppermute | solution.py:42
  171.6 8.4 %collective-permute-start.36 = (f32[1,64,512]{2,1,0:T(8,128)}, f32[1,64,512]{2,1,0:T(8,128)}, u32[]{:S(2)}, u32[]{:S(2)}) collective-permute-start(f32[1,64,512]{2,1,0:T(8,128)} %add.56), channel_id=1, source_target_pairs={{0,192},{1,65},{2,194},{3,67},{4,196},{5,69},{6,198},{7,71},{8,200... | collective-permute-start | bytes 393224 | tf_op jit(solution)/shard_map/ppermute | solution.py:42
  181.0 19.5 %collective-permute-start.37 = (bf16[4,2,176,256]{3,2,1,0:T(8,128)(2,1)}, bf16[4,2,176,256]{3,2,1,0:T(8,128)(2,1)S(1)}, u32[]{:S(2)}, u32[]{:S(2)}) collective-permute-start(bf16[4,2,176,256]{3,2,1,0:T(8,128)(2,1)} %get-tuple-element.187), channel_id=1, source_target_pairs={{0,4},{1,13},{2,6},{3,15},{4,0},{5,9},{6,2},{7,11},{8,12},{9,5},{1... | collective-permute-start | bytes 2162696 | tf_op jit(solution)/shard_map/ppermute | solution.py:42
  183.9 16.5 %collective-permute-start.38 = (bf16[4,2,80,256]{3,2,1,0:T(8,128)(2,1)}, bf16[4,2,80,256]{3,2,1,0:T(8,128)(2,1)S(1)}, u32[]{:S(2)}, u32[]{:S(2)}) collective-permute-start(bf16[4,2,80,256]{3,2,1,0:T(8,128)(2,1)} %get-tuple-element.188), channel_id=1, source_target_pairs={{0,2},{1,3},{2,0},{3,1},{4,6},{5,7},{6,4},{7,5},{8,10},{9,11},{10,... | collective-permute-start | bytes 983048 | tf_op jit(solution)/shard_map/ppermute | solution.py:42
  202.1 10.2 %collective-permute-start.41 = (bf16[2,2,176,256]{3,2,1,0:T(8,128)(2,1)S(1)}, bf16[2,2,176,256]{3,2,1,0:T(8,128)(2,1)S(1)}, u32[]{:S(2)}, u32[]{:S(2)}) collective-permute-start(bf16[2,2,176,256]{3,2,1,0:T(8,128)(2,1)S(1)} %get-tuple-element.195), channel_id=1, source_target_pairs={{0,12},{1,5},{2,14},{3,7},{4,8},{5,1},{6,10},{7,3},{8,4},{9,13},{1... | collective-permute-start | bytes 1081352 | tf_op jit(solution)/shard_map/ppermute | solution.py:42
  212.4 14.0 %collective-permute-start.47 = (f32[4,64,512]{2,1,0:T(8,128)S(1)}, f32[4,64,512]{2,1,0:T(8,128)S(1)}, u32[]{:S(2)}, u32[]{:S(2)}) collective-permute-start(f32[4,64,512]{2,1,0:T(8,128)S(1)} %pad_maximum_fusion.7), channel_id=1, source_target_pairs={{0,4},{1,13},{2,6},{3,15},{4,0},{5,9},{6,2},{7,11},{8,12},{9,5},{1... | collective-permute-start | bytes 1572872 | tf_op jit(solution)/shard_map/ppermute | solution.py:42
  216.4 10.1 %collective-permute-start.45 = (bf16[1,2,176,256]{3,2,1,0:T(8,128)(2,1)S(1)}, bf16[1,2,176,256]{3,2,1,0:T(8,128)(2,1)S(1)}, u32[]{:S(2)}, u32[]{:S(2)}) collective-permute-start(bf16[1,2,176,256]{3,2,1,0:T(8,128)(2,1)S(1)} %get-tuple-element.204), channel_id=1, source_target_pairs={{0,2},{1,3},{2,0},{3,1},{4,6},{5,7},{6,4},{7,5},{8,10},{9,11},{10,... | collective-permute-start | bytes 540680 | tf_op jit(solution)/shard_map/ppermute | solution.py:42
  217.3 9.2 %collective-permute-start.46 = (bf16[1,2,80,256]{3,2,1,0:T(8,128)(2,1)S(1)}, bf16[1,2,80,256]{3,2,1,0:T(8,128)(2,1)S(1)}, u32[]{:S(2)}, u32[]{:S(2)}) collective-permute-start(bf16[1,2,80,256]{3,2,1,0:T(8,128)(2,1)S(1)} %get-tuple-element.207), channel_id=1, source_target_pairs={{0,12},{1,5},{2,14},{3,7},{4,8},{5,1},{6,10},{7,3},{8,4},{9,13},{1... | collective-permute-start | bytes 245768 | tf_op jit(solution)/shard_map/ppermute | solution.py:42
  226.5 11.9 %collective-permute-start.49 = (f32[8,64,512]{2,1,0:T(8,128)S(1)}, f32[8,64,512]{2,1,0:T(8,128)S(1)}, u32[]{:S(2)}, u32[]{:S(2)}) collective-permute-start(f32[8,64,512]{2,1,0:T(8,128)S(1)} %pad_maximum_fusion.2.mine), channel_id=1, source_target_pairs={{0,1},{1,0},{2,3},{3,2},{4,5},{5,4},{6,7},{7,6},{8,9},{9,8},{10,11... | collective-permute-start | bytes 3145736 | tf_op jit(solution)/shard_map/ppermute | solution.py:42
  (42 other events, 383.0 us)
